TPU v7x, 32 devices: a whole 2x2x4 slice. The times are simulated.
32 devices in a mesh: groups: 2 (over y), tenant: 4 (over z), out: 2 (over x), inp: 2 (over core).
Axes of the slice: x: 2, y: 2, z: 4, core: 2. Of those that a mesh axis runs over, the one named last changes fastest.
Arguments:
- acts: bfloat16 [2048, 8192], P(('groups', 'tenant'), ('out', 'inp')), parts along dimension 0, may hold values from -6 to 6
- saved_projections: bfloat16 [2048, 2, 14336], P(('groups', 'tenant'), None, ('out', 'inp')), parts along dimension 0, may hold values from -8 to 8
- hidden_gradient: bfloat16 [2048, 14336], P(('groups', 'tenant'), ('out', 'inp')), parts along dimension 0, may hold values from -6 to 6
- adapter_down_weight: bfloat16 [16, 16, 8192], P(('groups', 'tenant'), None, ('out', 'inp')), parts along dimension 0, may hold values from -0.0625 to 0.0625
- adapter_up_weight: bfloat16 [16, 16, 2, 14336], P(('groups', 'tenant'), None, None, ('out', 'inp')), parts along dimension 0, may hold values from -0.0625 to 0.0625
- adapter_per_block: int32 [64], P(('groups', 'tenant')), parts along dimension 0, may hold values from 0 to 7, as said below
Outputs:
- grad_acts: bfloat16 [2048, 8192], P(('groups', 'tenant'), ('out', 'inp')), parts along dimension 0
- grad_a: float32 [16, 16, 8192], P(('groups', 'tenant'), None, ('out', 'inp')), parts along dimension 0
- grad_b: float32 [16, 16, 2, 14336], P(('groups', 'tenant'), None, None, ('out', 'inp')), parts along dimension 0
There are 2 independent parts, one for each index of `groups`. A program takes and returns all parts, laid end to end along the dimension named above; each array names one. Nothing has to cross between parts.
Inputs may be any that keep to these rules, and one draw needn't show every extreme that they name: `adapter_per_block`: adapter a is held by tenant index a // 2. The 8 blocks of one tenant index name adapters of all different holders where there are no more blocks than tenant indices, else every holder at least once; they never name two different adapters held by the same tenant index, but may name one adapter more than once.
All inputs are finite; a program needn't handle non-finite values.
Results may differ from a plain program's by a relative error of at most 0.0058.
Values may be sent and summed in bfloat16 or wider, within the bound.
No kernel may reach another device: no remote copies, remote signals or barrier semaphores. Data moves between devices by JAX's collectives and lax.ppermute only.
A program may use at most 64 MiB of HBM per device.

v0:
```python
import jax
import jax.numpy as jnp
from jax import lax
from jax.sharding import PartitionSpec as P

adapter_scale = 2.0


def swiglu_back(saved_projections, hidden_gradient):
    gate_part = saved_projections[:, 0].astype(jnp.float32)
    up_part = saved_projections[:, 1].astype(jnp.float32)
    hidden_grad = hidden_gradient.astype(jnp.float32)
    sigma_gate = jax.nn.sigmoid(gate_part)
    grad_gate = hidden_grad * up_part * sigma_gate * (1.0 + gate_part * (1.0 - sigma_gate))
    grad_up = hidden_grad * gate_part * sigma_gate
    return jnp.stack([grad_gate, grad_up], axis=1).astype(jnp.bfloat16)


def on_device(
    acts,
    saved_projections,
    hidden_gradient,
    adapter_down_weight,
    adapter_up_weight,
    adapter_per_block,
):
    tenant_count = lax.axis_size("tenant")
    own_index = lax.axis_index("tenant")
    blocks_here = adapter_per_block.shape[0]
    local_adapters = adapter_down_weight.shape[0]
    row_count = acts.shape[0]
    block_rows = row_count // blocks_here
    width_here = acts.shape[1]
    units_here = saved_projections.shape[2]
    grad_proj = swiglu_back(saved_projections, hidden_gradient)
    all_ids = lax.all_gather(adapter_per_block, "tenant", axis=0, tiled=True)
    peer_ids = all_ids.reshape(tenant_count, blocks_here)
    is_mine = peer_ids // local_adapters == own_index
    local_slot = peer_ids % local_adapters
    slot_range = jnp.arange(local_adapters, dtype=jnp.int32)
    wanted = jnp.any(
        is_mine[:, :, None] & (local_slot[:, :, None] == slot_range[None, None, :]), axis=1
    )
    wanted_bf = wanted.astype(jnp.bfloat16)
    holder_of = adapter_per_block // local_adapters
    holder_hot = holder_of[:, None] == jnp.arange(tenant_count, dtype=jnp.int32)[None, :]
    down_fragment = lax.all_gather(adapter_down_weight, "tenant", axis=0, tiled=True)
    up_fragment = lax.all_gather(adapter_up_weight, "tenant", axis=0, tiled=True)
    piece_count = down_fragment.shape[0]
    matches = (
        adapter_per_block[:, None] == jnp.arange(piece_count, dtype=jnp.int32)[None, :]
    ).astype(jnp.bfloat16)
    found_a = jnp.einsum(
        "kj,jrd->krd", matches, down_fragment, preferred_element_type=jnp.float32
    ).astype(jnp.bfloat16)
    found_b = jnp.einsum(
        "kj,jrqf->krqf", matches, up_fragment, preferred_element_type=jnp.float32
    ).astype(jnp.bfloat16)
    act_blocks = acts.reshape(blocks_here, block_rows, width_here)
    proj_blocks = grad_proj.reshape(blocks_here, block_rows, 2, units_here)
    in_part = jnp.einsum("ktd,krd->ktr", act_blocks, found_a, preferred_element_type=jnp.float32)
    out_part = jnp.einsum(
        "ktjf,krjf->ktr", proj_blocks, found_b, preferred_element_type=jnp.float32
    )
    low_in, low_out = lax.psum((in_part, out_part), ("out", "inp"))
    rank_input = low_in.astype(jnp.bfloat16)
    rank_output = low_out.astype(jnp.bfloat16)
    input_gradient = adapter_scale * jnp.einsum(
        "bmh,bhc->bmc", rank_output, found_a, preferred_element_type=jnp.float32
    )
    grad_acts = input_gradient.astype(jnp.bfloat16).reshape(row_count, width_here)
    down_portion = adapter_scale * jnp.einsum(
        "mqj,mqh->mhj", act_blocks, rank_output, preferred_element_type=jnp.float32
    )
    up_portion = adapter_scale * jnp.einsum(
        "zly,zlds->zyds", rank_input, proj_blocks, preferred_element_type=jnp.float32
    )
    holder_wide = holder_hot.astype(jnp.float32)
    back_a = jnp.einsum(
        "kp,krd->prd", holder_wide, down_portion, precision=lax.Precision.HIGHEST
    ).astype(jnp.bfloat16)
    back_b = jnp.einsum(
        "kp,krjf->prjf", holder_wide, up_portion, precision=lax.Precision.HIGHEST
    ).astype(jnp.bfloat16)
    came_a, came_b = (
        lax.all_to_all(back_a, "tenant", split_axis=0, concat_axis=0, tiled=True),
        lax.all_to_all(back_b, "tenant", split_axis=0, concat_axis=0, tiled=True),
    )
    grad_a = jnp.einsum("pc,prd->crd", wanted_bf, came_a, preferred_element_type=jnp.float32)
    grad_b = jnp.einsum("pc,prjf->crjf", wanted_bf, came_b, preferred_element_type=jnp.float32)
    return (grad_acts, grad_a, grad_b)


def solution(mesh):
    return jax.shard_map(
        on_device,
        mesh=mesh,
        in_specs=(
            P(("groups", "tenant"), ("out", "inp")),
            P(("groups", "tenant"), None, ("out", "inp")),
            P(("groups", "tenant"), ("out", "inp")),
            P(("groups", "tenant"), None, ("out", "inp")),
            P(("groups", "tenant"), None, None, ("out", "inp")),
            P(("groups", "tenant")),
        ),
        out_specs=(
            P(("groups", "tenant"), ("out", "inp")),
            P(("groups", "tenant"), None, ("out", "inp")),
            P(("groups", "tenant"), None, None, ("out", "inp")),
        ),
        check_vma=False,
    )
```

profile of v0, /device:TPU:0, one launch (start us, length us, event | category | flops | bytes accessed | tf_op | source)
XLA Modules:
  0.0 130.1 jit_solution(2258522045372731421)
XLA Ops:
  7.2 0.0 copy-start
  7.2 0.0 copy-start.3
  7.2 0.0 all-gather.2.cloned.1.call-start
  7.2 1.9 %copy.26 = bf16[2,16,2,3584]{3,1,2,0:T(8,128)(2,1)} copy(bf16[2,16,2,3584]{3,2,1,0:T(2,128)(2,1)} %param.10) | data formatting | bytes 917504 | tf_op args[4]
  9.1 0.0 all-gather.2.cloned.1.call-update
  9.2 20.4 %all_gather.10 = bf16[8,16,2048]{2,1,0:T(8,128)(2,1)S(1)} all-gather(bf16[2,16,2048]{2,1,0:T(8,128)(2,1)} %param.9), channel_id=1, replica_groups=mesh['groups'=2,'tenant'=4,'out'=2,'inp'=2] {'tenant'}, dimensions={0}, use_global_device_ids=true | all-gather | bytes 655360 | tf_op jit(solution)/shard_map/all_gather | solution.py:47
  29.6 1.1 convolution_convert_fusion.2
  30.7 0.0 copy-done
  30.7 0.5 convolution_bitcast_fusion
  31.2 0.0 copy-done.3
  31.3 0.0 copy-start.2
  31.3 7.8 %fusion.49 = (bf16[256,1,3584]{2,1,0:T(2,128)(2,1)S(1)}, bf16[256,1,3584]{2,1,0:T(2,128)(2,1)S(1)}) fusion(bf16[256,2,3584]{2,1,0:T(2,128)(2,1)} %param.7), kind=kLoop, calls=%fused_computation.72 | loop fusion | bytes 7340032 | tf_op jit(solution)/shard_map/slice | solution.py:11
  39.1 0.0 copy-done.2
  39.1 2.9 %fusion.2 = (bf16[256,3584]{1,0:T(8,128)(2,1)S(1)}, bf16[256,3584]{1,0:T(8,128)(2,1)}) fusion(bf16[256,3584]{1,0:T(8,128)(2,1)S(1)} %copy-done.2, bf16[256,1,3584]{2,1,0:T(2,128)(2,1)S(1)} %get-tuple-element.16, bf16[256,1,3584]{2,1,0:T(2,128)(2,1)S(1)} %get-tuple-element.17), kind=kLoop, calls=%fused_computation.9 | loop fusion | flops 14680064 | bytes 9175040 | tf_op jit(solution)/shard_map/convert.5
  42.0 14.5 %all-gather.2.cloned.1.call-done = bf16[8,16,2,3584]{3,1,2,0:T(8,128)(2,1)} async-done(((bf16[2,16,2,3584]{3,1,2,0:T(8,128)(2,1)}), bf16[8,16,2,3584]{3,1,2,0:T(8,128)(2,1)}) %all-gather.2.cloned.1.call-update) | async-done | bytes 1835024 | tf_op jit(solution)/shard_map/all_gather | solution.py:48
  56.5 0.0 copy-start.1
  56.5 3.7 %convolution_convert_fusion = bf16[8,16,2,3584]{3,0,2,1:T(8,128)(2,1)S(1)} fusion(bf16[8,16,2,3584]{3,1,2,0:T(8,128)(2,1)} %all-gather.2.cloned.1.call-done, s32[8]{0:T(128)S(1)} %copy-done.3), kind=kOutput, calls=%fused_computation.4 | convolution fusion | flops 15597632 | bytes 3670048 | tf_op jit(solution)/shard_map/kj,jrqf->krqf/dot_general | solution.py:56
  60.2 0.0 copy-done.1
  60.3 2.1 %fusion.14 = f32[8,32,16]{1,2,0:T(8,128)} fusion(bf16[8,16,2,3584]{3,0,2,1:T(8,128)(2,1)S(1)} %convolution_convert_fusion, bf16[8,32,1,3584]{3,1,2,0:T(8,128)(2,1)S(1)} %bitcast.60, bf16[8,32,1,3584]{3,1,2,0:T(8,128)(2,1)S(1)} %bitcast.57), kind=kOutput, calls=%fused_computation.29 | convolution fusion | flops 60555264 | bytes 5521408 | tf_op jit(solution)/shard_map/ktjf,krjf->ktr/dot_general | solution.py:62
  62.4 12.4 %all-reduce.1 = (bf16[8,32,16]{1,2,0:T(8,128)(2,1)S(1)}, bf16[8,32,16]{1,2,0:T(8,128)(2,1)S(1)}) all-reduce(f32[8,32,16]{1,2,0:T(8,128)} %fusion.14, f32[8,32,16]{1,2,0:T(8,128)S(1)} %convolution_bitcast_fusion), channel_id=1, replica_groups=mesh['groups'=2,'tenant'=4,'out'=2,'inp'=2] {'out','inp'}, use_global_device_ids=true, to_apply=%region_0.1 | all-reduce | flops 8192 | bytes 49152 | tf_op jit(solution)/shard_map/psum | solution.py:65
  74.7 0.3 convolution_multiply_fusion.2
  75.0 1.2 convolution_convert_fusion.3
  76.2 0.9 copy.32
  77.1 4.2 %all-to-all-start = ((bf16[4,16,2048]{2,1,0:T(8,128)(2,1)}), bf16[4,16,2048]{2,1,0:T(8,128)(2,1)}, u32[]{:S(2)}, u32[]{:S(2)}) async-start(bf16[4,16,2048]{2,1,0:T(8,128)(2,1)} %copy.32), calls=%async_computation | async-start | bytes 524288 | tf_op jit(solution)/shard_map/all_to_all | solution.py:86
  81.3 2.1 %convolution_multiply_fusion = f32[8,16,2,3584]{3,1,2,0:T(8,128)S(1)} fusion(bf16[8,32,1,3584]{3,1,2,0:T(8,128)(2,1)} %bitcast.59, bf16[8,32,1,3584]{3,1,2,0:T(8,128)(2,1)S(1)} %bitcast.58, bf16[8,32,16]{1,2,0:T(8,128)(2,1)S(1)} %get-tuple-element.13), kind=kOutput, calls=%fused_computation | convolution fusion | flops 66977792 | bytes 7348224 | tf_op jit(solution)/shard_map/zly,zlds->zyds/dot_general | solution.py:75
  83.4 0.0 copy-start.4
  83.4 3.8 %convolution_convert_fusion.1 = bf16[4,16,2,3584]{3,0,2,1:T(4,128)(2,1)S(1)} fusion(f32[8,16,2,3584]{3,1,2,0:T(8,128)S(1)} %convolution_multiply_fusion, s32[8]{0:T(128)S(1)} %and_select_fusion), kind=kOutput, calls=%fused_computation.5 | convolution fusion | flops 44498976 | bytes 4587552 | tf_op jit(solution)/shard_map/kp,krjf->prjf/dot_general | solution.py:82
  87.3 1.6 %copy.36 = bf16[4,16,2,3584]{3,2,1,0:T(2,128)(2,1)} copy(bf16[4,16,2,3584]{3,0,2,1:T(4,128)(2,1)S(1)} %convolution_convert_fusion.1) | data formatting | bytes 1835008 | tf_op jit(solution)/shard_map/convert_element_type | solution.py:84
  88.9 1.7 %all-to-all-done = bf16[4,16,2048]{2,1,0:T(8,128)(2,1)} async-done(((bf16[4,16,2048]{2,1,0:T(8,128)(2,1)}), bf16[4,16,2048]{2,1,0:T(8,128)(2,1)}, u32[]{:S(2)}, u32[]{:S(2)}) %all-to-all-start) | async-done | bytes 262176 | tf_op jit(solution)/shard_map/all_to_all | solution.py:86
  90.6 3.5 %all-to-all-start.1 = ((bf16[4,16,2,3584]{3,2,1,0:T(2,128)(2,1)}), bf16[4,16,2,3584]{3,2,1,0:T(2,128)(2,1)S(1)}, u32[]{:S(2)}, u32[]{:S(2)}) async-start(bf16[4,16,2,3584]{3,2,1,0:T(2,128)(2,1)} %copy.36), calls=%async_computation.1 | async-start | bytes 1835008 | tf_op jit(solution)/shard_map/all_to_all | solution.py:87
  94.1 0.0 copy-done.4
  94.2 0.6 dynamic-slice
  95.4 0.2 dynamic-update-slice
  95.6 21.3 %all-reduce = s32[32]{0:T(128)S(1)} all-reduce(s32[32]{0:T(128)S(1)} %dynamic-update-slice), channel_id=1, replica_groups=mesh['groups'=2,'tenant'=4,'out'=2,'inp'=2] {'tenant'}, use_global_device_ids=true, to_apply=%add | all-reduce | flops 32 | bytes 256
  116.9 0.1 reshape.79
  117.0 0.1 fusion.34
  117.2 1.7 %fusion.10 = bf16[8,32,2048]{2,1,0:T(8,128)(2,1)} fusion(bf16[8,16,2048]{2,0,1:T(8,128)(2,1)S(1)} %convolution_convert_fusion.2, bf16[8,32,16]{1,2,0:T(8,128)(2,1)S(1)} %get-tuple-element.12), kind=kOutput, calls=%fused_computation.19 | convolution fusion | flops 17825792 | bytes 1581056 | tf_op jit(solution)/shard_map/bmh,bhc->bmc/dot_general | solution.py:68
  118.9 1.2 fusion.23
  120.1 0.9 copy.38
  121.0 0.0 all-to-all-done.1
  121.0 0.9 fusion.18
  121.8 1.4 %copy.39 = f32[2,16,2,3584]{3,2,1,0:T(2,128)} copy(f32[2,16,2,3584]{3,0,2,1:T(2,128)S(1)} %fusion.18) | data formatting | bytes 1835008
  (4 shorter events, 0.0 us)
Async XLA Ops:
  7.2 23.6 %copy-start = (bf16[256,2048]{1,0:T(8,128)(2,1)S(1)}, bf16[256,2048]{1,0:T(8,128)(2,1)}, u32[]{:S(2)}) copy-start(bf16[256,2048]{1,0:T(8,128)(2,1)} %param.6) | copy-start | bytes 3145732
  7.2 24.1 %copy-start.3 = (s32[8]{0:T(128)S(1)}, s32[8]{0:T(128)}, u32[]{:S(2)}) copy-start(s32[8]{0:T(128)} %param.11) | copy-start | bytes 100
  7.2 49.3 %all-gather.2.cloned.1.call-start = ((), (), s32[]{:S(2)}) async-start(), calls=%async_computation.2 | async-start | bytes 2293760 | tf_op jit(solution)/shard_map/all_gather | solution.py:48
  31.3 7.8 %copy-start.2 = (bf16[256,3584]{1,0:T(8,128)(2,1)S(1)}, bf16[256,3584]{1,0:T(8,128)(2,1)}, u32[]{:S(2)}) copy-start(bf16[256,3584]{1,0:T(8,128)(2,1)} %param.8) | copy-start | bytes 5505028
  56.5 3.7 %copy-start.1 = (bf16[256,3584]{1,0:T(8,128)(2,1)S(1)}, bf16[256,3584]{1,0:T(8,128)(2,1)}, u32[]{:S(2)}) copy-start(bf16[256,3584]{1,0:T(8,128)(2,1)} %get-tuple-element.15) | copy-start | bytes 5505028
  77.1 13.6 %all-to-all-start = ((bf16[4,16,2048]{2,1,0:T(8,128)(2,1)}), bf16[4,16,2048]{2,1,0:T(8,128)(2,1)}, u32[]{:S(2)}, u32[]{:S(2)}) async-start(bf16[4,16,2048]{2,1,0:T(8,128)(2,1)} %copy.32), calls=%async_computation | async-start | bytes 524288 | tf_op jit(solution)/shard_map/all_to_all | solution.py:86
  83.4 10.7 %copy-start.4 = (u32[32]{0:T(128)S(1)}, u32[32]{0:T(128)}, u32[]{:S(2)}) copy-start(u32[32]{0:T(128)} %constant.52) | copy-start | bytes 388
  90.6 30.4 %all-to-all-start.1 = ((bf16[4,16,2,3584]{3,2,1,0:T(2,128)(2,1)}), bf16[4,16,2,3584]{3,2,1,0:T(2,128)(2,1)S(1)}, u32[]{:S(2)}, u32[]{:S(2)}) async-start(bf16[4,16,2,3584]{3,2,1,0:T(2,128)(2,1)} %copy.36), calls=%async_computation.1 | async-start | bytes 1835008 | tf_op jit(solution)/shard_map/all_to_all | solution.py:87
Sparse Core Ops, SparseCore 0:
  10.2 46.2 all-gather.1
where the time goes:
time: 131 us; the launch traced here: 130 us
  blocking collectives  54.1 us (41%)
  matrix products  18.7 us (14%)
  waiting for transfers between devices  16.2 us (12%)
  local copies, waits for them, and re-layouts  15.4 us (12%)
  between operations  14.9 us (11%)
  starting transfers between devices  7.78 us (6%)
  other arithmetic  3.08 us (2%)
    unnamed x1, blocking collectives  21.3 us
    all_gather x1, blocking collectives, on_device(): lax.all_gather(adapter_down_weight, 'tenant', axis=0, tiled=True)  20.4 us
    all_gather x1, waiting for transfers between devices, on_device(): lax.all_gather(adapter_up_weight, 'tenant', axis=0, tiled=True)  14.5 us
    psum x1, blocking collectives, on_device(): low_in, low_out = lax.psum((in_part, out_part), ('out', 'inp'))  12.4 us
    slice x1, local copies, waits for them, and re-layouts, swiglu_back(): up_part = saved_projections[:, 1].astype(jnp.float32)  7.79 us
    unnamed x16, local copies, waits for them, and re-layouts  5.02 us
    all_to_all x1, starting transfers between devices, on_device(): lax.all_to_all(back_a, 'tenant', split_axis=0, concat_axis=0, tiled=True)  4.23 us
    dot_general x1, matrix products, on_device(): jnp.einsum('kp,krjf->prjf', holder_wide, up_portion, precision=lax.Precis...  3.85 us
  transfers between devices with their start and end apart: 3, of which 2 were waited for; matrix products, arithmetic and copies ran while one was open for 19% of the time, Pallas kernels for 0%

commit v1 on v0

v1 whole, which is shorter than its diff:
```python
import functools

import jax
import jax.numpy as jnp
from jax import lax
from jax.experimental import pallas as pl
from jax.experimental.pallas import tpu as pltpu
from jax.sharding import PartitionSpec as P

adapter_scale = 2.0
BF = jnp.bfloat16
F32 = jnp.float32
COST = 1


def dot(a, b, ca, cb):
    return lax.dot_general(a, b, (((ca,), (cb,)), ((), ())), preferred_element_type=F32)


def on_chip(body, outs, scratch=(), vmem=16 << 20):
    return pl.pallas_call(
        body,
        out_shape=outs,
        scratch_shapes=list(scratch),
        compiler_params=pltpu.CompilerParams(vmem_limit_bytes=vmem),
        cost_estimate=pl.CostEstimate(flops=COST, bytes_accessed=COST, transcendentals=0),
    )


def asked_slot(ids, slots):
    me = lax.axis_index("tenant")
    return jnp.max(jnp.where(lax.div(ids, slots) == me, lax.rem(ids, slots), 0))


def peer_index(k, count):
    return lax.rem(lax.axis_index("tenant") + k, count)


def choose(count, slots, *refs):
    ids, down, up = refs[:count], refs[count], refs[count + 1]
    outs = refs[count + 2 :]
    for k in range(count):
        asked = asked_slot(ids[k][...], slots)
        outs[k][...] = down[asked]
        outs[count + k][...] = up[asked]


def keep_own(full, row_holder, count, rank):
    total = jnp.zeros((rank, full.shape[1]), F32)
    for k in range(count):
        own = row_holder == peer_index(k, count)
        total = total + jnp.where(own, full[k * rank : (k + 1) * rank], 0.0)
    return total


def rank_in(count, rank, row_holder, acts, *refs):
    down, out, stack = refs[:count], refs[count], refs[count + 1]
    for k in range(count):
        stack[pl.ds(k * rank, rank), :] = down[k][...]
    out[...] = keep_own(dot(stack[...], acts[...], 1, 1), row_holder[...], count, rank)


def rank_out(count, rank, row_holder, gate, up, *refs):
    maps, out, stack = refs[:count], refs[count], refs[count + 1]
    for k in range(count):
        for j in range(2):
            stack[j, pl.ds(k * rank, rank), :] = maps[k][j]
    full = dot(stack[0], gate[...], 1, 1) + dot(stack[1], up[...], 1, 1)
    out[...] = keep_own(full, row_holder[...], count, rank)


def fill_wide(wide, row_holder, low, count, rank):
    narrow = low.astype(BF).astype(F32)
    for k in range(count):
        own = row_holder == peer_index(k, count)
        wide[pl.ds(k * rank, rank), :] = jnp.where(own, narrow, 0.0).astype(BF)


def parts_b(count, rank, row_holder, low, more, gate, up, *refs):
    outs, wide = refs[:count], refs[count]
    fill_wide(wide, row_holder[...], low[...] + more[...], count, rank)
    for j, grad in enumerate((gate, up)):
        part = (adapter_scale * dot(wide[...], grad[...], 1, 0)).astype(BF)
        for k in range(count):
            outs[k][j] = part[k * rank : (k + 1) * rank]


def parts_a(count, rank, row_holder, low, more, acts, *refs):
    outs, wide = refs[:count], refs[count]
    fill_wide(wide, row_holder[...], low[...] + more[...], count, rank)
    part = (adapter_scale * dot(wide[...], acts[...], 1, 0)).astype(BF)
    for k in range(count):
        outs[k][...] = part[k * rank : (k + 1) * rank]


def input_grad(count, rank, row_holder, low, more, *refs):
    down, out, stack, wide = refs[:count], refs[count], refs[count + 1], refs[count + 2]
    fill_wide(wide, row_holder[...], low[...] + more[...], count, rank)
    for k in range(count):
        stack[pl.ds(k * rank, rank), :] = down[k][...]
    out[...] = (adapter_scale * dot(wide[...], stack[...], 0, 0)).astype(BF)


def held_sum_a(count, slots, *refs):
    ids, parts, out = refs[:count], refs[count : 2 * count], refs[2 * count]
    asked = [asked_slot(ids[k][...], slots) for k in range(count)]
    for a in range(slots):
        total = jnp.zeros(parts[0].shape, F32)
        for k in range(count):
            total = total + jnp.where(asked[k] == a, parts[k][...].astype(F32), 0.0)
        out[a] = total


def held_sum_b(count, slots, *refs):
    ids, parts, out = refs[:count], refs[count : 2 * count], refs[2 * count]
    asked = [asked_slot(ids[k][...], slots) for k in range(count)]
    for a in range(slots):
        for j in range(2):
            total = jnp.zeros(parts[0].shape[1:], F32)
            for k in range(count):
                total = total + jnp.where(asked[k] == a, parts[k][j].astype(F32), 0.0)
            out[a, :, j, :] = total


def on_device(acts, saved, hidden, down, up, ids):
    T = lax.axis_size("tenant")
    slots, rank, width = down.shape
    units = up.shape[3]
    rows = acts.shape[0]
    block_rows = rows // ids.shape[0]
    every = range(T)
    shape = jax.ShapeDtypeStruct

    def shift(x, k):
        return lax.ppermute(x, "tenant", [(i, (i + k) % T) for i in range(T)])

    order = sorted(range(1, T), key=lambda k: -min(k, T - k))

    ids_from = {0: ids}
    for k in order:
        ids_from[k] = shift(ids, k)
    ids_from = [ids_from[k].reshape(1, -1) for k in every]

    up_by_gate = jnp.swapaxes(up, 1, 2)
    sends = on_chip(
        functools.partial(choose, T, slots),
        [shape((rank, width), BF)] * T + [shape((2, rank, units), BF)] * T,
    )(*ids_from, down, up_by_gate)
    sends, saved, hidden = lax.optimization_barrier((sends, saved, hidden))
    down_from, up_from = {0: sends[0]}, {0: sends[T]}
    for k in order:
        down_from[k] = shift(sends[k], -k)
    for k in order:
        up_from[k] = shift(sends[T + k], -k)
    down_from = [down_from[k] for k in every]
    up_from = [up_from[k] for k in every]

    saved_by_gate = jnp.swapaxes(saved, 0, 1)
    g = saved_by_gate[0].astype(F32)
    u = saved_by_gate[1].astype(F32)
    h = hidden.astype(F32)
    s = jax.nn.sigmoid(g)
    grad_gate = (h * u * s * (1.0 + g * (1.0 - s))).astype(BF)
    grad_up = (h * g * s).astype(BF)

    row_holder = jnp.repeat(ids // slots, block_rows).reshape(1, rows)

    def feature_sum(x):
        for axis in ("inp", "out"):
            n = lax.axis_size(axis)
            rest = [lax.ppermute(x, axis, [(i, (i + k) % n) for i in range(n)]) for k in range(1, n)]
            more = sum(rest[1:], rest[0]) if rest else jnp.zeros_like(x)
            if axis == "inp":
                x = x + more
        return x, more

    part = functools.partial
    low_in = on_chip(
        part(rank_in, T, rank),
        shape((rank, rows), F32),
        [pltpu.VMEM((T * rank, width), BF)],
    )(row_holder, acts, *down_from)
    low_in, more_in = feature_sum(low_in)
    back_b = on_chip(
        part(parts_b, T, rank),
        [shape((2, rank, units), BF)] * T,
        [pltpu.VMEM((T * rank, rows), BF)],
    )(row_holder, low_in, more_in, grad_gate, grad_up)

    low_out = on_chip(
        part(rank_out, T, rank),
        shape((rank, rows), F32),
        [pltpu.VMEM((2, T * rank, units), BF)],
    )(row_holder, grad_gate, grad_up, *up_from)
    low_out, more_out = feature_sum(low_out)
    back_a = on_chip(
        part(parts_a, T, rank),
        [shape((rank, width), BF)] * T,
        [pltpu.VMEM((T * rank, rows), BF)],
    )(row_holder, low_out, more_out, acts)
    grad_acts = on_chip(
        part(input_grad, T, rank),
        shape((rows, width), BF),
        [pltpu.VMEM((T * rank, width), BF), pltpu.VMEM((T * rank, rows), BF)],
    )(row_holder, low_out, more_out, *down_from)

    got_b = {0: back_b[0]}
    for k in order:
        got_b[k] = shift(back_b[k], k)
    got_a = {0: back_a[0]}
    for k in order:
        got_a[k] = shift(back_a[k], k)
    grad_b = on_chip(
        part(held_sum_b, T, slots),
        shape((slots, rank, 2, units), F32),
    )(*ids_from, *[got_b[k] for k in every])
    grad_a = on_chip(
        part(held_sum_a, T, slots),
        shape((slots, rank, width), F32),
    )(*ids_from, *[got_a[k] for k in every])
    return grad_acts, grad_a, grad_b


def solution(mesh):
    row = ("groups", "tenant")
    col = ("out", "inp")
    return jax.shard_map(
        on_device,
        mesh=mesh,
        in_specs=(
            P(row, col),
            P(row, None, col),
            P(row, col),
            P(row, None, col),
            P(row, None, None, col),
            P(row),
        ),
        out_specs=(
            P(row, col),
            P(row, None, col),
            P(row, None, None, col),
        ),
        check_vma=False,
    )
```

time: 131 us -> 73.2 us (0.56)
  blocking collectives: 54.1 us -> 0 us
  matrix products: 18.7 us -> 0 us
  starting transfers between devices: 7.78 us -> 25.9 us
  waiting for transfers between devices: 16.2 us -> 30.7 us
  between operations: 14.9 us -> 0.77 us
  local copies, waits for them, and re-layouts: 15.4 us -> 6.53 us
  Pallas kernels: 0 us -> 7.14 us
    ppermute x0 -> x19, waiting for transfers between devices: none -> 30.7 us  [the longest x15 27 us: shift(): return lax.ppermute(x, 'tenant', [(i, (i + k) % T) for i in range(T)])]
    ppermute x0 -> x19, starting transfers between devices: none -> 25.9 us  [the longest x15 22.7 us: shift(): return lax.ppermute(x, 'tenant', [(i, (i + k) % T) for i in range(T)])]
    unnamed x1 -> x0, blocking collectives: 21.3 us -> none
    all_gather x1 -> x0, blocking collectives: 20.4 us -> none  [on_device(): lax.all_gather(adapter_down_weight, 'tenant', axis=0, tiled=True)]
    dot_general x11 -> x0, matrix products: 18.7 us -> none  [the longest x1 3.85 us: on_device(): jnp.einsum('kp,krjf->prjf', holder_wide, up_portion, precision=lax.Precis...]
    all_gather x1 -> x0, waiting for transfers between devices: 14.5 us -> none  [on_device(): lax.all_gather(adapter_up_weight, 'tenant', axis=0, tiled=True)]
    psum x1 -> x0, blocking collectives: 12.4 us -> none  [on_device(): low_in, low_out = lax.psum((in_part, out_part), ('out', 'inp'))]
    slice x1 -> x0, local copies, waits for them, and re-layouts: 7.79 us -> none  [swiglu_back(): up_part = saved_projections[:, 1].astype(jnp.float32)]
  transfers between devices with their start and end apart: 3 -> 19, of which waited for: 2 -> 9; matrix products, arithmetic and copies ran while one was open for 19% -> 8% of each run, Pallas kernels for 0% -> 7%
where the time goes in v1:
time: 73.2 us; the launch traced here: 73 us
  waiting for transfers between devices  30.7 us (42%)
  starting transfers between devices  25.9 us (35%)
  Pallas kernels  7.14 us (10%)
  local copies, waits for them, and re-layouts  6.53 us (9%)
  other arithmetic  1.94 us (3%)
  between operations  0.77 us (1%)
    ppermute x15, waiting for transfers between devices, shift(): return lax.ppermute(x, 'tenant', [(i, (i + k) % T) for i in range(T)])  27 us
    ppermute x15, starting transfers between devices, shift(): return lax.ppermute(x, 'tenant', [(i, (i + k) % T) for i in range(T)])  22.7 us
    unnamed x13, local copies, waits for them, and re-layouts  3.86 us
    ppermute x4, waiting for transfers between devices, feature_sum(): lax.ppermute(x, axis, [(i, (i + k) % n) for i in range(n)])  3.73 us
    ppermute x4, starting transfers between devices, feature_sum(): lax.ppermute(x, axis, [(i, (i + k) % n) for i in range(n)])  3.18 us
    optimization_barrier x1, local copies, waits for them, and re-layouts, on_device(): sends, saved, hidden = lax.optimization_barrier((sends, saved, hidden))  2.52 us
    convert_element_type x1, other arithmetic, on_device(): grad_up = (h * g * s).astype(BF)  1.92 us
    pallas_call x1, Pallas kernels, on_device(): on_chip(part(held_sum_b, T, slots), shape((slots, rank, 2, units), F32))  1.7 us
  transfers between devices with their start and end apart: 19, of which 9 were waited for; matrix products, arithmetic and copies ran while one was open for 8% of the time, Pallas kernels for 7%

profile of v1, /device:TPU:0, one launch (start us, length us, event | category | flops | bytes accessed | tf_op | source)
XLA Modules:
  0.0 73.0 jit_solution(4020232584298483709)
XLA Ops:
  0.6 3.1 %collective-permute-start = (s32[8]{0:T(128)}, s32[8]{0:T(128)S(1)}, u32[]{:S(2)}, u32[]{:S(2)}) collective-permute-start(s32[8]{0:T(128)} %param.11), channel_id=1, source_target_pairs={{0,4},{4,8},{8,12},{12,0},{1,5},{5,9},{9,13},{13,1},{2,6},{6,10},{... | collective-permute-start | bytes 104 | tf_op jit(solution)/shard_map/ppermute | solution.py:135
  3.7 2.6 %collective-permute-start.1 = (s32[8]{0:T(128)}, s32[8]{0:T(128)S(1)}, u32[]{:S(2)}, u32[]{:S(2)}) collective-permute-start(s32[8]{0:T(128)} %param.11), channel_id=1, source_target_pairs={{0,8},{4,12},{8,0},{12,4},{1,9},{5,13},{9,1},{13,5},{2,10},{6,14},... | collective-permute-start | bytes 104 | tf_op jit(solution)/shard_map/ppermute | solution.py:135
  6.3 1.3 %collective-permute-start.2 = (s32[8]{0:T(128)}, s32[8]{0:T(128)S(1)}, u32[]{:S(2)}, u32[]{:S(2)}) collective-permute-start(s32[8]{0:T(128)} %param.11), channel_id=1, source_target_pairs={{0,12},{4,0},{8,4},{12,8},{1,13},{5,1},{9,5},{13,9},{2,14},{6,2},{... | collective-permute-start | bytes 104 | tf_op jit(solution)/shard_map/ppermute | solution.py:135
  7.6 1.1 %copy.14 = bf16[2,16,2,3584]{3,1,2,0:T(8,128)(2,1)S(1)} copy(bf16[2,16,2,3584]{3,2,1,0:T(2,128)(2,1)} %param.10) | data formatting | bytes 917504 | tf_op args[4]
  8.7 0.0 collective-permute-done.1
  8.7 1.2 %collective-permute-done.2 = s32[8]{0:T(128)S(1)} collective-permute-done((s32[8]{0:T(128)}, s32[8]{0:T(128)S(1)}, u32[]{:S(2)}, u32[]{:S(2)}) %collective-permute-start.2) | collective-permute-done | bytes 64 | tf_op jit(solution)/shard_map/ppermute | solution.py:135
  10.0 0.9 %copy-done.2 = bf16[2,16,2048]{2,1,0:T(8,128)(2,1)S(1)} copy-done((bf16[2,16,2048]{2,1,0:T(8,128)(2,1)S(1)}, bf16[2,16,2048]{2,1,0:T(8,128)(2,1)}, u32[]{:S(2)}) %copy-start.2) | copy-done | bytes 131096
  10.9 0.7 copy-done.3
  11.5 0.3 shard_map.85
  11.8 3.2 %collective-permute-start.8 = (bf16[16,2048]{1,0:T(8,128)(2,1)S(1)}, bf16[16,2048]{1,0:T(8,128)(2,1)S(1)}, u32[]{:S(2)}, u32[]{:S(2)}) collective-permute-start(bf16[16,2048]{1,0:T(8,128)(2,1)S(1)} %get-tuple-element.44), channel_id=1, source_target_pairs={{0,12},{4,0},{8,4},{12,8},{1,13},{5,1},{9,5},{13,9},{2,14},{6,2},{... | collective-permute-start | bytes 196616 | tf_op jit(solution)/shard_map/ppermute | solution.py:135
  15.0 0.6 collective-permute-start.10
  15.7 0.1 broadcast_in_dim.3
  15.7 0.1 reshape_reshape.3.row_holder
  15.8 1.1 %collective-permute-done.8.refs_1_ = bf16[16,2048]{1,0:T(8,128)(2,1)S(1)} collective-permute-done((bf16[16,2048]{1,0:T(8,128)(2,1)S(1)}, bf16[16,2048]{1,0:T(8,128)(2,1)S(1)}, u32[]{:S(2)}, u32[]{:S(2)}) %collective-permute-start.8) | collective-permute-done | bytes 65568 | tf_op jit(solution)/shard_map/ppermute | solution.py:135
  16.9 3.3 %collective-permute-done.9.refs_2_ = bf16[16,2048]{1,0:T(8,128)(2,1)S(1)} collective-permute-done((bf16[16,2048]{1,0:T(8,128)(2,1)S(1)}, bf16[16,2048]{1,0:T(8,128)(2,1)S(1)}, u32[]{:S(2)}, u32[]{:S(2)}) %collective-permute-start.9) | collective-permute-done | bytes 65568 | tf_op jit(solution)/shard_map/ppermute | solution.py:135
  20.2 0.9 %collective-permute-done.10.refs_3_ = bf16[16,2048]{1,0:T(8,128)(2,1)S(1)} collective-permute-done((bf16[16,2048]{1,0:T(8,128)(2,1)S(1)}, bf16[16,2048]{1,0:T(8,128)(2,1)S(1)}, u32[]{:S(2)}, u32[]{:S(2)}) %collective-permute-start.10) | collective-permute-done | bytes 65568 | tf_op jit(solution)/shard_map/ppermute | solution.py:135
  21.1 1.2 %copy-done = bf16[256,2048]{1,0:T(8,128)(2,1)S(1)} copy-done((bf16[256,2048]{1,0:T(8,128)(2,1)S(1)}, bf16[256,2048]{1,0:T(8,128)(2,1)}, u32[]{:S(2)}) %copy-start) | copy-done | bytes 1048600
  22.3 0.4 shard_map.90
  22.8 0.1 collective-permute-start.14
  22.9 2.5 %copy.13 = bf16[256,2,3584]{2,0,1:T(8,128)(2,1)S(1)} copy(bf16[256,2,3584]{2,1,0:T(2,128)(2,1)} %param.7) | data formatting | bytes 7340032 | tf_op jit(solution)/shard_map/optimization_barrier | solution.py:149
  25.4 0.8 %collective-permute-start.3 = (bf16[2,16,3584]{2,1,0:T(8,128)(2,1)S(1)}, bf16[2,16,3584]{2,1,0:T(8,128)(2,1)S(1)}, u32[]{:S(2)}, u32[]{:S(2)}) collective-permute-start(bf16[2,16,3584]{2,1,0:T(8,128)(2,1)S(1)} %get-tuple-element.40), channel_id=1, source_target_pairs={{0,12},{4,0},{8,4},{12,8},{1,13},{5,1},{9,5},{13,9},{2,14},{6,2},{... | collective-permute-start | bytes 688136 | tf_op jit(solution)/shard_map/ppermute | solution.py:135
  26.2 0.5 collective-permute-start.4
  26.6 1.9 %collective-permute-start.5 = (bf16[2,16,3584]{2,1,0:T(8,128)(2,1)S(1)}, bf16[2,16,3584]{2,1,0:T(8,128)(2,1)S(1)}, u32[]{:S(2)}, u32[]{:S(2)}) collective-permute-start(bf16[2,16,3584]{2,1,0:T(8,128)(2,1)S(1)} %get-tuple-element.42), channel_id=1, source_target_pairs={{0,4},{4,8},{8,12},{12,0},{1,5},{5,9},{9,13},{13,1},{2,6},{6,10},{... | collective-permute-start | bytes 688136 | tf_op jit(solution)/shard_map/ppermute | solution.py:135
  28.6 1.6 %collective-permute-start.15 = (f32[16,256]{1,0:T(8,128)S(1)}, f32[16,256]{1,0:T(8,128)S(1)}, u32[]{:S(2)}, u32[]{:S(2)}) collective-permute-start(f32[16,256]{1,0:T(8,128)S(1)} %add.16.low), channel_id=1, source_target_pairs={{0,2},{2,0},{1,3},{3,1},{4,6},{6,4},{5,7},{7,5},{8,10},{10,8},{9,1... | collective-permute-start | bytes 49160 | tf_op jit(solution)/shard_map/ppermute | solution.py:171
  30.1 1.9 %fusion.8 = (bf16[256,3584]{1,0:T(8,128)(2,1)S(1)}, bf16[256,3584]{1,0:T(8,128)(2,1)S(1)}) fusion(bf16[256,3584]{1,0:T(8,128)(2,1)S(1)} %copy-done.5, bf16[2,256,3584]{2,1,0:T(8,128)(2,1)S(1)} %bitcast.35), kind=kLoop, calls=%fused_computation.12 | loop fusion | flops 14680064 | bytes 9175040 | tf_op jit(solution)/shard_map/convert_element_type | solution.py:164
  32.1 0.3 collective-permute-done.15.more
  32.4 0.8 %shard_map.91 = (bf16[2,16,3584]{2,1,0:T(8,128)(2,1)S(1)}, bf16[2,16,3584]{2,1,0:T(8,128)(2,1)S(1)}, bf16[2,16,3584]{2,1,0:T(8,128)(2,1)S(1)}, bf16[2,16,3584]{2,1,0:T(8,128)(2,1)S(1)}) custom-call(s32[1,256]{1,0:T(1,128)S(1)} %reshape_reshape.3.row_holder, f32[16,256]{1,0:T(8,128)S(1)} %add.16.low, f32[16,256]{1,0:T(8,128)S(1)} %collective-permute-done.15.more, ...), custom_call_target="tpu_custom_call" | custom-call | flops 1 | bytes 1 | tf_op jit(solution)/shard_map/pallas_call | solution.py:184
  33.2 0.0 copy-start.4
  33.2 1.1 %collective-permute-start.16 = (bf16[2,16,3584]{2,1,0:T(8,128)(2,1)S(1)}, bf16[2,16,3584]{2,1,0:T(8,128)(2,1)S(1)}, u32[]{:S(2)}, u32[]{:S(2)}) collective-permute-start(bf16[2,16,3584]{2,1,0:T(8,128)(2,1)S(1)} %get-tuple-element.52), channel_id=1, source_target_pairs={{0,4},{4,8},{8,12},{12,0},{1,5},{5,9},{9,13},{13,1},{2,6},{6,10},{... | collective-permute-start | bytes 688136 | tf_op jit(solution)/shard_map/ppermute | solution.py:135
  34.3 1.4 %collective-permute-start.17 = (bf16[2,16,3584]{2,1,0:T(8,128)(2,1)S(1)}, bf16[2,16,3584]{2,1,0:T(8,128)(2,1)S(1)}, u32[]{:S(2)}, u32[]{:S(2)}) collective-permute-start(bf16[2,16,3584]{2,1,0:T(8,128)(2,1)S(1)} %get-tuple-element.53), channel_id=1, source_target_pairs={{0,8},{4,12},{8,0},{12,4},{1,9},{5,13},{9,1},{13,5},{2,10},{6,14},... | collective-permute-start | bytes 688136 | tf_op jit(solution)/shard_map/ppermute | solution.py:135
  35.7 0.0 collective-permute-done.3.refs_1_
  35.7 2.3 %collective-permute-start.18 = (bf16[2,16,3584]{2,1,0:T(8,128)(2,1)S(1)}, bf16[2,16,3584]{2,1,0:T(8,128)(2,1)S(1)}, u32[]{:S(2)}, u32[]{:S(2)}) collective-permute-start(bf16[2,16,3584]{2,1,0:T(8,128)(2,1)S(1)} %get-tuple-element.54), channel_id=1, source_target_pairs={{0,12},{4,0},{8,4},{12,8},{1,13},{5,1},{9,5},{13,9},{2,14},{6,2},{... | collective-permute-start | bytes 688136 | tf_op jit(solution)/shard_map/ppermute | solution.py:135
  38.0 19.7 %collective-permute-done.4.refs_2_ = bf16[2,16,3584]{2,1,0:T(8,128)(2,1)S(1)} collective-permute-done((bf16[2,16,3584]{2,1,0:T(8,128)(2,1)S(1)}, bf16[2,16,3584]{2,1,0:T(8,128)(2,1)S(1)}, u32[]{:S(2)}, u32[]{:S(2)}) %collective-permute-start.4) | collective-permute-done | bytes 229408 | tf_op jit(solution)/shard_map/ppermute | solution.py:135
  57.6 0.0 collective-permute-done.5.refs_3_
  57.6 1.2 %shard_map.86 = f32[16,256]{1,0:T(8,128)S(1)} custom-call(s32[1,256]{1,0:T(1,128)S(1)} %reshape_reshape.3.row_holder, bf16[256,3584]{1,0:T(8,128)(2,1)S(1)} %get-tuple-element.56.gate, bf16[256,3584]{1,0:T(8,128)(2,1)S(1)} %get-tuple-element.55.up, bf16[2,16,3584]{2,1,0:T(8,128)(2,1)S(1)} %get-tuple-element.39.refs_0_, ...), custom_call_target="tpu_custom_call" | custom-call | flops 1 | bytes 1 | tf_op jit(solution)/shard_map/pallas_call | solution.py:190
  58.9 0.1 collective-permute-start.6
  58.9 1.2 %collective-permute-done.6 = f32[16,256]{1,0:T(8,128)S(1)} collective-permute-done((f32[16,256]{1,0:T(8,128)S(1)}, f32[16,256]{1,0:T(8,128)S(1)}, u32[]{:S(2)}, u32[]{:S(2)}) %collective-permute-start.6) | collective-permute-done | bytes 16416 | tf_op jit(solution)/shard_map/ppermute | solution.py:171
  60.1 1.5 %collective-permute-start.7 = (f32[16,256]{1,0:T(8,128)S(1)}, f32[16,256]{1,0:T(8,128)S(1)}, u32[]{:S(2)}, u32[]{:S(2)}) collective-permute-start(f32[16,256]{1,0:T(8,128)S(1)} %add.15.low), channel_id=1, source_target_pairs={{0,2},{2,0},{1,3},{3,1},{4,6},{6,4},{5,7},{7,5},{8,10},{10,8},{9,1... | collective-permute-start | bytes 49160 | tf_op jit(solution)/shard_map/ppermute | solution.py:171
  61.6 2.2 %collective-permute-done.7.more = f32[16,256]{1,0:T(8,128)S(1)} collective-permute-done((f32[16,256]{1,0:T(8,128)S(1)}, f32[16,256]{1,0:T(8,128)S(1)}, u32[]{:S(2)}, u32[]{:S(2)}) %collective-permute-start.7) | collective-permute-done | bytes 16416 | tf_op jit(solution)/shard_map/ppermute | solution.py:171
  63.8 0.3 shard_map.88
  64.2 0.1 collective-permute-start.11
  64.2 0.1 collective-permute-start.12
  64.3 0.0 collective-permute-done.16.refs_5_
  64.3 3.7 %collective-permute-start.13 = (bf16[16,2048]{1,0:T(8,128)(2,1)S(1)}, bf16[16,2048]{1,0:T(8,128)(2,1)S(1)}, u32[]{:S(2)}, u32[]{:S(2)}) collective-permute-start(bf16[16,2048]{1,0:T(8,128)(2,1)S(1)} %get-tuple-element.50), channel_id=1, source_target_pairs={{0,12},{4,0},{8,4},{12,8},{1,13},{5,1},{9,5},{13,9},{2,14},{6,2},{... | collective-permute-start | bytes 196616 | tf_op jit(solution)/shard_map/ppermute | solution.py:135
  68.0 1.4 %shard_map.87 = bf16[256,2048]{1,0:T(8,128)(2,1)} custom-call(s32[1,256]{1,0:T(1,128)S(1)} %reshape_reshape.3.row_holder, f32[16,256]{1,0:T(8,128)S(1)} %add.15.low, f32[16,256]{1,0:T(8,128)S(1)} %collective-permute-done.7.more, bf16[16,2048]{1,0:T(8,128)(2,1)S(1)} %get-tuple-element.43.refs_0_, bf16[16,2048]{1,0:T(8,128)(2,1)S(1)} %collective-permute-done.8.refs_1_, ...), custom_call_target="tpu_custom_call" | custom-call | flops 1 | bytes 1 | tf_op jit(solution)/shard_map/pallas_call | solution.py:201
  69.5 1.7 %shard_map.92 = f32[2,16,2,3584]{3,2,1,0:T(2,128)} custom-call(s32[1,8]{1,0:T(1,128)S(1)} %bitcast.24, s32[1,8]{1,0:T(1,128)S(1)} %bitcast.27, s32[1,8]{1,0:T(1,128)S(1)} %bitcast.30, s32[1,8]{1,0:T(1,128)S(1)} %bitcast.33, bf16[2,16,3584]{2,1,0:T(8,128)(2,1)S(1)} %get-tuple-element.51.refs_4_, bf16[2,16,3584]{2,1,0:T(8,128)(2,1)S(1)} %collective-permute-done.16.refs_5_, ...), custom_call_target="tpu_custom_call" | custom-call | flops 1 | bytes 1 | tf_op jit(solution)/shard_map/pallas_call | solution.py:213
  71.2 0.8 %collective-permute-done.12.refs_6_ = bf16[16,2048]{1,0:T(8,128)(2,1)S(1)} collective-permute-done((bf16[16,2048]{1,0:T(8,128)(2,1)S(1)}, bf16[16,2048]{1,0:T(8,128)(2,1)S(1)}, u32[]{:S(2)}, u32[]{:S(2)}) %collective-permute-start.12) | collective-permute-done | bytes 65568 | tf_op jit(solution)/shard_map/ppermute | solution.py:135
  72.0 1.0 %shard_map.89 = f32[2,16,2048]{2,1,0:T(8,128)} custom-call(s32[1,8]{1,0:T(1,128)S(1)} %bitcast.25, s32[1,8]{1,0:T(1,128)S(1)} %bitcast.28, s32[1,8]{1,0:T(1,128)S(1)} %bitcast.31, s32[1,8]{1,0:T(1,128)S(1)} %bitcast.34, bf16[16,2048]{1,0:T(8,128)(2,1)S(1)} %get-tuple-element.47.refs_4_, bf16[16,2048]{1,0:T(8,128)(2,1)S(1)} %collective-permute-done.11.refs_5_, ...), custom_call_target="tpu_custom_call" | custom-call | flops 1 | bytes 1 | tf_op jit(solution)/shard_map/pallas_call | solution.py:217
  (18 shorter events, 0.0 us)
Async XLA Ops:
  0.6 8.1 %collective-permute-start = (s32[8]{0:T(128)}, s32[8]{0:T(128)S(1)}, u32[]{:S(2)}, u32[]{:S(2)}) collective-permute-start(s32[8]{0:T(128)} %param.11), channel_id=1, source_target_pairs={{0,4},{4,8},{8,12},{12,0},{1,5},{5,9},{9,13},{13,1},{2,6},{6,10},{... | collective-permute-start | bytes 104 | tf_op jit(solution)/shard_map/ppermute | solution.py:135
  3.7 5.0 %collective-permute-start.1 = (s32[8]{0:T(128)}, s32[8]{0:T(128)S(1)}, u32[]{:S(2)}, u32[]{:S(2)}) collective-permute-start(s32[8]{0:T(128)} %param.11), channel_id=1, source_target_pairs={{0,8},{4,12},{8,0},{12,4},{1,9},{5,13},{9,1},{13,5},{2,10},{6,14},... | collective-permute-start | bytes 104 | tf_op jit(solution)/shard_map/ppermute | solution.py:135
  6.3 3.7 %collective-permute-start.2 = (s32[8]{0:T(128)}, s32[8]{0:T(128)S(1)}, u32[]{:S(2)}, u32[]{:S(2)}) collective-permute-start(s32[8]{0:T(128)} %param.11), channel_id=1, source_target_pairs={{0,12},{4,0},{8,4},{12,8},{1,13},{5,1},{9,5},{13,9},{2,14},{6,2},{... | collective-permute-start | bytes 104 | tf_op jit(solution)/shard_map/ppermute | solution.py:135
  10.0 0.9 %copy-start.2 = (bf16[2,16,2048]{2,1,0:T(8,128)(2,1)S(1)}, bf16[2,16,2048]{2,1,0:T(8,128)(2,1)}, u32[]{:S(2)}) copy-start(bf16[2,16,2048]{2,1,0:T(8,128)(2,1)} %refs_4_.1) | copy-start | bytes 393220
  10.9 0.7 copy-start.3
  11.8 5.1 %collective-permute-start.8 = (bf16[16,2048]{1,0:T(8,128)(2,1)S(1)}, bf16[16,2048]{1,0:T(8,128)(2,1)S(1)}, u32[]{:S(2)}, u32[]{:S(2)}) collective-permute-start(bf16[16,2048]{1,0:T(8,128)(2,1)S(1)} %get-tuple-element.44), channel_id=1, source_target_pairs={{0,12},{4,0},{8,4},{12,8},{1,13},{5,1},{9,5},{13,9},{2,14},{6,2},{... | collective-permute-start | bytes 196616 | tf_op jit(solution)/shard_map/ppermute | solution.py:135
  15.0 5.2 %collective-permute-start.9 = (bf16[16,2048]{1,0:T(8,128)(2,1)S(1)}, bf16[16,2048]{1,0:T(8,128)(2,1)S(1)}, u32[]{:S(2)}, u32[]{:S(2)}) collective-permute-start(bf16[16,2048]{1,0:T(8,128)(2,1)S(1)} %get-tuple-element.45), channel_id=1, source_target_pairs={{0,8},{4,12},{8,0},{12,4},{1,9},{5,13},{9,1},{13,5},{2,10},{6,14},... | collective-permute-start | bytes 196616 | tf_op jit(solution)/shard_map/ppermute | solution.py:135
  15.0 6.1 %collective-permute-start.10 = (bf16[16,2048]{1,0:T(8,128)(2,1)S(1)}, bf16[16,2048]{1,0:T(8,128)(2,1)S(1)}, u32[]{:S(2)}, u32[]{:S(2)}) collective-permute-start(bf16[16,2048]{1,0:T(8,128)(2,1)S(1)} %get-tuple-element.46), channel_id=1, source_target_pairs={{0,4},{4,8},{8,12},{12,0},{1,5},{5,9},{9,13},{13,1},{2,6},{6,10},{... | collective-permute-start | bytes 196616 | tf_op jit(solution)/shard_map/ppermute | solution.py:135
  21.1 1.2 %copy-start = (bf16[256,2048]{1,0:T(8,128)(2,1)S(1)}, bf16[256,2048]{1,0:T(8,128)(2,1)}, u32[]{:S(2)}) copy-start(bf16[256,2048]{1,0:T(8,128)(2,1)} %acts.3) | copy-start | bytes 3145732
  22.8 7.4 %copy-start.5 = (bf16[256,3584]{1,0:T(8,128)(2,1)S(1)}, bf16[256,3584]{1,0:T(8,128)(2,1)}, u32[]{:S(2)}) copy-start(bf16[256,3584]{1,0:T(8,128)(2,1)} %param.8) | copy-start | bytes 5505028
  22.8 5.8 %collective-permute-start.14 = (f32[16,256]{1,0:T(8,128)S(1)}, f32[16,256]{1,0:T(8,128)S(1)}, u32[]{:S(2)}, u32[]{:S(2)}) collective-permute-start(f32[16,256]{1,0:T(8,128)S(1)} %shard_map.90), channel_id=1, source_target_pairs={{0,1},{1,0},{2,3},{3,2},{4,5},{5,4},{6,7},{7,6},{8,9},{9,8},{10,11... | collective-permute-start | bytes 49160 | tf_op jit(solution)/shard_map/ppermute | solution.py:171
  25.4 10.3 %collective-permute-start.3 = (bf16[2,16,3584]{2,1,0:T(8,128)(2,1)S(1)}, bf16[2,16,3584]{2,1,0:T(8,128)(2,1)S(1)}, u32[]{:S(2)}, u32[]{:S(2)}) collective-permute-start(bf16[2,16,3584]{2,1,0:T(8,128)(2,1)S(1)} %get-tuple-element.40), channel_id=1, source_target_pairs={{0,12},{4,0},{8,4},{12,8},{1,13},{5,1},{9,5},{13,9},{2,14},{6,2},{... | collective-permute-start | bytes 688136 | tf_op jit(solution)/shard_map/ppermute | solution.py:135
  26.2 31.5 %collective-permute-start.4 = (bf16[2,16,3584]{2,1,0:T(8,128)(2,1)S(1)}, bf16[2,16,3584]{2,1,0:T(8,128)(2,1)S(1)}, u32[]{:S(2)}, u32[]{:S(2)}) collective-permute-start(bf16[2,16,3584]{2,1,0:T(8,128)(2,1)S(1)} %get-tuple-element.41), channel_id=1, source_target_pairs={{0,8},{4,12},{8,0},{12,4},{1,9},{5,13},{9,1},{13,5},{2,10},{6,14},... | collective-permute-start | bytes 688136 | tf_op jit(solution)/shard_map/ppermute | solution.py:135
  26.6 31.0 %collective-permute-start.5 = (bf16[2,16,3584]{2,1,0:T(8,128)(2,1)S(1)}, bf16[2,16,3584]{2,1,0:T(8,128)(2,1)S(1)}, u32[]{:S(2)}, u32[]{:S(2)}) collective-permute-start(bf16[2,16,3584]{2,1,0:T(8,128)(2,1)S(1)} %get-tuple-element.42), channel_id=1, source_target_pairs={{0,4},{4,8},{8,12},{12,0},{1,5},{5,9},{9,13},{13,1},{2,6},{6,10},{... | collective-permute-start | bytes 688136 | tf_op jit(solution)/shard_map/ppermute | solution.py:135
  28.6 3.8 %collective-permute-start.15 = (f32[16,256]{1,0:T(8,128)S(1)}, f32[16,256]{1,0:T(8,128)S(1)}, u32[]{:S(2)}, u32[]{:S(2)}) collective-permute-start(f32[16,256]{1,0:T(8,128)S(1)} %add.16.low), channel_id=1, source_target_pairs={{0,2},{2,0},{1,3},{3,1},{4,6},{6,4},{5,7},{7,5},{8,10},{10,8},{9,1... | collective-permute-start | bytes 49160 | tf_op jit(solution)/shard_map/ppermute | solution.py:171
  32.4 31.5 %copy-start.1 = (bf16[256,2048]{1,0:T(8,128)(2,1)S(1)}, bf16[256,2048]{1,0:T(8,128)(2,1)}, u32[]{:S(2)}) copy-start(bf16[256,2048]{1,0:T(8,128)(2,1)} %acts.3) | copy-start | bytes 3145732
  33.2 36.3 %copy-start.4 = (s32[8]{0:T(128)S(1)}, s32[8]{0:T(128)}, u32[]{:S(2)}) copy-start(s32[8]{0:T(128)} %param.11) | copy-start | bytes 100
  33.2 31.1 %collective-permute-start.16 = (bf16[2,16,3584]{2,1,0:T(8,128)(2,1)S(1)}, bf16[2,16,3584]{2,1,0:T(8,128)(2,1)S(1)}, u32[]{:S(2)}, u32[]{:S(2)}) collective-permute-start(bf16[2,16,3584]{2,1,0:T(8,128)(2,1)S(1)} %get-tuple-element.52), channel_id=1, source_target_pairs={{0,4},{4,8},{8,12},{12,0},{1,5},{5,9},{9,13},{13,1},{2,6},{6,10},{... | collective-permute-start | bytes 688136 | tf_op jit(solution)/shard_map/ppermute | solution.py:135
  34.3 35.2 %collective-permute-start.17 = (bf16[2,16,3584]{2,1,0:T(8,128)(2,1)S(1)}, bf16[2,16,3584]{2,1,0:T(8,128)(2,1)S(1)}, u32[]{:S(2)}, u32[]{:S(2)}) collective-permute-start(bf16[2,16,3584]{2,1,0:T(8,128)(2,1)S(1)} %get-tuple-element.53), channel_id=1, source_target_pairs={{0,8},{4,12},{8,0},{12,4},{1,9},{5,13},{9,1},{13,5},{2,10},{6,14},... | collective-permute-start | bytes 688136 | tf_op jit(solution)/shard_map/ppermute | solution.py:135
  35.7 33.8 %collective-permute-start.18 = (bf16[2,16,3584]{2,1,0:T(8,128)(2,1)S(1)}, bf16[2,16,3584]{2,1,0:T(8,128)(2,1)S(1)}, u32[]{:S(2)}, u32[]{:S(2)}) collective-permute-start(bf16[2,16,3584]{2,1,0:T(8,128)(2,1)S(1)} %get-tuple-element.54), channel_id=1, source_target_pairs={{0,12},{4,0},{8,4},{12,8},{1,13},{5,1},{9,5},{13,9},{2,14},{6,2},{... | collective-permute-start | bytes 688136 | tf_op jit(solution)/shard_map/ppermute | solution.py:135
  58.9 1.2 %collective-permute-start.6 = (f32[16,256]{1,0:T(8,128)S(1)}, f32[16,256]{1,0:T(8,128)S(1)}, u32[]{:S(2)}, u32[]{:S(2)}) collective-permute-start(f32[16,256]{1,0:T(8,128)S(1)} %shard_map.86), channel_id=1, source_target_pairs={{0,1},{1,0},{2,3},{3,2},{4,5},{5,4},{6,7},{7,6},{8,9},{9,8},{10,11... | collective-permute-start | bytes 49160 | tf_op jit(solution)/shard_map/ppermute | solution.py:171
  60.1 3.7 %collective-permute-start.7 = (f32[16,256]{1,0:T(8,128)S(1)}, f32[16,256]{1,0:T(8,128)S(1)}, u32[]{:S(2)}, u32[]{:S(2)}) collective-permute-start(f32[16,256]{1,0:T(8,128)S(1)} %add.15.low), channel_id=1, source_target_pairs={{0,2},{2,0},{1,3},{3,1},{4,6},{6,4},{5,7},{7,5},{8,10},{10,8},{9,1... | collective-permute-start | bytes 49160 | tf_op jit(solution)/shard_map/ppermute | solution.py:171
  64.2 7.0 %collective-permute-start.11 = (bf16[16,2048]{1,0:T(8,128)(2,1)S(1)}, bf16[16,2048]{1,0:T(8,128)(2,1)S(1)}, u32[]{:S(2)}, u32[]{:S(2)}) collective-permute-start(bf16[16,2048]{1,0:T(8,128)(2,1)S(1)} %get-tuple-element.48), channel_id=1, source_target_pairs={{0,4},{4,8},{8,12},{12,0},{1,5},{5,9},{9,13},{13,1},{2,6},{6,10},{... | collective-permute-start | bytes 196616 | tf_op jit(solution)/shard_map/ppermute | solution.py:135
  64.2 7.8 %collective-permute-start.12 = (bf16[16,2048]{1,0:T(8,128)(2,1)S(1)}, bf16[16,2048]{1,0:T(8,128)(2,1)S(1)}, u32[]{:S(2)}, u32[]{:S(2)}) collective-permute-start(bf16[16,2048]{1,0:T(8,128)(2,1)S(1)} %get-tuple-element.49), channel_id=1, source_target_pairs={{0,8},{4,12},{8,0},{12,4},{1,9},{5,13},{9,1},{13,5},{2,10},{6,14},... | collective-permute-start | bytes 196616 | tf_op jit(solution)/shard_map/ppermute | solution.py:135
  64.3 7.7 %collective-permute-start.13 = (bf16[16,2048]{1,0:T(8,128)(2,1)S(1)}, bf16[16,2048]{1,0:T(8,128)(2,1)S(1)}, u32[]{:S(2)}, u32[]{:S(2)}) collective-permute-start(bf16[16,2048]{1,0:T(8,128)(2,1)S(1)} %get-tuple-element.50), channel_id=1, source_target_pairs={{0,12},{4,0},{8,4},{12,8},{1,13},{5,1},{9,5},{13,9},{2,14},{6,2},{... | collective-permute-start | bytes 196616 | tf_op jit(solution)/shard_map/ppermute | solution.py:135

commit v2 on v1

--- a/solution.py
+++ b/solution.py
@@ -17,11 +17,12 @@
     return lax.dot_general(a, b, (((ca,), (cb,)), ((), ())), preferred_element_type=F32)
 
 
-def on_chip(body, outs, scratch=(), vmem=16 << 20):
+def on_chip(body, outs, scratch=(), vmem=16 << 20, **blocks):
     return pl.pallas_call(
         body,
         out_shape=outs,
         scratch_shapes=list(scratch),
+        **blocks,
         compiler_params=pltpu.CompilerParams(vmem_limit_bytes=vmem),
         cost_estimate=pl.CostEstimate(flops=COST, bytes_accessed=COST, transcendentals=0),
     )
@@ -34,6 +35,24 @@
 
 def peer_index(k, count):
     return lax.rem(lax.axis_index("tenant") + k, count)
+
+
+def bring(ids, down, up, ids_out, down_out, up_out, arrived):
+    pairs = ((ids, ids_out), (down, down_out), (up, up_out))
+    copies = [pltpu.make_async_copy(a, b, arrived.at[i]) for i, (a, b) in enumerate(pairs)]
+    for copy in copies:
+        copy.start()
+    for copy in copies:
+        copy.wait()
+
+
+def gated_grad(saved, hidden, gate, up):
+    g = saved[0].astype(F32)
+    u = saved[1].astype(F32)
+    h = hidden[...].astype(F32)
+    s = jax.nn.sigmoid(g)
+    gate[...] = (h * u * s * (1.0 + g * (1.0 - s))).astype(BF)
+    up[...] = (h * g * s).astype(BF)
 
 
 def choose(count, slots, *refs):
@@ -141,11 +160,18 @@
         ids_from[k] = shift(ids, k)
     ids_from = [ids_from[k].reshape(1, -1) for k in every]
 
-    up_by_gate = jnp.swapaxes(up, 1, 2)
+    own_ids = ids.reshape(1, -1)
+    own_ids, own_down, own_up = on_chip(
+        bring,
+        [shape(own_ids.shape, ids.dtype), shape(down.shape, BF), shape(up.shape, BF)],
+        [pltpu.SemaphoreType.DMA((3,))],
+        in_specs=[pl.BlockSpec(memory_space=pl.ANY)] * 3,
+    )(own_ids, down, up)
+    ids_from[0] = own_ids
     sends = on_chip(
         functools.partial(choose, T, slots),
-        [shape((rank, width), BF)] * T + [shape((2, rank, units), BF)] * T,
-    )(*ids_from, down, up_by_gate)
+        [shape((rank, width), BF)] * T + [shape((rank, 2, units), BF)] * T,
+    )(*ids_from, own_down, own_up)
     sends, saved, hidden = lax.optimization_barrier((sends, saved, hidden))
     down_from, up_from = {0: sends[0]}, {0: sends[T]}
     for k in order:
@@ -153,15 +179,19 @@
     for k in order:
         up_from[k] = shift(sends[T + k], -k)
     down_from = [down_from[k] for k in every]
-    up_from = [up_from[k] for k in every]
+    up_from = [jnp.swapaxes(up_from[k], 0, 1) for k in every]
 
     saved_by_gate = jnp.swapaxes(saved, 0, 1)
-    g = saved_by_gate[0].astype(F32)
-    u = saved_by_gate[1].astype(F32)
-    h = hidden.astype(F32)
-    s = jax.nn.sigmoid(g)
-    grad_gate = (h * u * s * (1.0 + g * (1.0 - s))).astype(BF)
-    grad_up = (h * g * s).astype(BF)
+    grad_gate, grad_up = on_chip(
+        gated_grad,
+        [shape((rows, units), BF)] * 2,
+        grid=(8,),
+        in_specs=[
+            pl.BlockSpec((2, rows // 8, units), lambda i: (0, i, 0)),
+            pl.BlockSpec((rows // 8, units), lambda i: (i, 0)),
+        ],
+        out_specs=[pl.BlockSpec((rows // 8, units), lambda i: (i, 0))] * 2,
+    )(saved_by_gate, hidden)
 
     row_holder = jnp.repeat(ids // slots, block_rows).reshape(1, rows)
 
@@ -175,6 +205,7 @@
         return x, more
 
     part = functools.partial
+    down_from, grad_gate, grad_up = lax.optimization_barrier((down_from, grad_gate, grad_up))
     low_in = on_chip(
         part(rank_in, T, rank),
         shape((rank, rows), F32),

time: 73.2 us -> 65.6 us (0.90)
  waiting for transfers between devices: 30.7 us -> 19.8 us
  starting transfers between devices: 25.9 us -> 29.4 us
  Pallas kernels: 7.14 us -> 9.92 us
  other arithmetic: 1.94 us -> 0.02 us
  local copies, waits for them, and re-layouts: 6.53 us -> 5.37 us
    ppermute x15, waiting for transfers between devices: 27 us -> 13 us  [shift(): return lax.ppermute(x, 'tenant', [(i, (i + k) % T) for i in range(T)])]
    ppermute x15, starting transfers between devices: 22.7 us -> 26.3 us  [shift(): return lax.ppermute(x, 'tenant', [(i, (i + k) % T) for i in range(T)])]
    ppermute x4, waiting for transfers between devices: 3.73 us -> 6.84 us  [feature_sum(): lax.ppermute(x, axis, [(i, (i + k) % n) for i in range(n)])]
    pallas_call x0 -> x2, Pallas kernels: none -> 2.76 us  [the longest x1 2.32 us: on_device(): on_chip(gated_grad, [shape((rows, units), BF)] * 2, grid=(8,), in_specs=[...]
    convert_element_type x1 -> x0, other arithmetic: 1.92 us -> none  [on_device(): grad_up = (h * g * s).astype(BF)]
    unnamed x13 -> x10, local copies, waits for them, and re-layouts: 3.86 us -> 2.58 us
    optimization_barrier x1 -> x5, local copies, waits for them, and re-layouts: 2.52 us -> 2.63 us  [on_device(): sends, saved, hidden = lax.optimization_barrier((sends, saved, hidden))]
  transfers between devices with their start and end apart: 19 -> 19, of which waited for: 9 -> 6; matrix products, arithmetic and copies ran while one was open for 8% -> 4% of each run, Pallas kernels for 7% -> 13%
where the time goes in v2:
time: 65.6 us; the launch traced here: 65.4 us
  starting transfers between devices  29.4 us (45%)
  waiting for transfers between devices  19.8 us (30%)
  Pallas kernels  9.92 us (15%)
  local copies, waits for them, and re-layouts  5.37 us (8%)
  between operations  0.82 us (1%)
    ppermute x15, starting transfers between devices, shift(): return lax.ppermute(x, 'tenant', [(i, (i + k) % T) for i in range(T)])  26.3 us
    ppermute x15, waiting for transfers between devices, shift(): return lax.ppermute(x, 'tenant', [(i, (i + k) % T) for i in range(T)])  13 us
    ppermute x4, waiting for transfers between devices, feature_sum(): lax.ppermute(x, axis, [(i, (i + k) % n) for i in range(n)])  6.84 us
    ppermute x4, starting transfers between devices, feature_sum(): lax.ppermute(x, axis, [(i, (i + k) % n) for i in range(n)])  3.12 us
    optimization_barrier x5, local copies, waits for them, and re-layouts, on_device(): sends, saved, hidden = lax.optimization_barrier((sends, saved, hidden))  2.63 us
    unnamed x10, local copies, waits for them, and re-layouts  2.58 us
    pallas_call x1, Pallas kernels, on_device(): on_chip(gated_grad, [shape((rows, units), BF)] * 2, grid=(8,), in_specs=[...  2.32 us
    pallas_call x1, Pallas kernels, on_device(): on_chip(part(held_sum_b, T, slots), shape((slots, rank, 2, units), F32))  1.7 us
  transfers between devices with their start and end apart: 19, of which 6 were waited for; matrix products, arithmetic and copies ran while one was open for 4% of the time, Pallas kernels for 13%

profile of v2, /device:TPU:0, one launch (start us, length us, event | category | flops | bytes accessed | tf_op | source)
XLA Modules:
  0.0 65.4 jit_solution(6888158230865712714)
XLA Ops:
  0.6 3.1 %collective-permute-start = (s32[8]{0:T(128)}, s32[8]{0:T(128)S(1)}, u32[]{:S(2)}, u32[]{:S(2)}) collective-permute-start(s32[8]{0:T(128)} %param.11), channel_id=1, source_target_pairs={{0,4},{4,8},{8,12},{12,0},{1,5},{5,9},{9,13},{13,1},{2,6},{6,10},{... | collective-permute-start | bytes 104 | tf_op jit(solution)/shard_map/ppermute | solution.py:154
  3.7 2.6 %collective-permute-start.1 = (s32[8]{0:T(128)}, s32[8]{0:T(128)S(1)}, u32[]{:S(2)}, u32[]{:S(2)}) collective-permute-start(s32[8]{0:T(128)} %param.11), channel_id=1, source_target_pairs={{0,8},{4,12},{8,0},{12,4},{1,9},{5,13},{9,1},{13,5},{2,10},{6,14},... | collective-permute-start | bytes 104 | tf_op jit(solution)/shard_map/ppermute | solution.py:154
  6.3 1.3 %collective-permute-start.2 = (s32[8]{0:T(128)}, s32[8]{0:T(128)S(1)}, u32[]{:S(2)}, u32[]{:S(2)}) collective-permute-start(s32[8]{0:T(128)} %param.11), channel_id=1, source_target_pairs={{0,12},{4,0},{8,4},{12,8},{1,13},{5,1},{9,5},{13,9},{2,14},{6,2},{... | collective-permute-start | bytes 104 | tf_op jit(solution)/shard_map/ppermute | solution.py:154
  7.6 1.0 %copy-done.2 = bf16[2,16,2,3584]{3,2,1,0:T(2,128)(2,1)S(1)} copy-done((bf16[2,16,2,3584]{3,2,1,0:T(2,128)(2,1)S(1)}, bf16[2,16,2,3584]{3,2,1,0:T(2,128)(2,1)}, u32[]{:S(2)}) %copy-start.2) | copy-done | bytes 458776
  8.7 0.9 %copy-done.3 = bf16[2,16,2048]{2,1,0:T(8,128)(2,1)S(1)} copy-done((bf16[2,16,2048]{2,1,0:T(8,128)(2,1)S(1)}, bf16[2,16,2048]{2,1,0:T(8,128)(2,1)}, u32[]{:S(2)}) %copy-start.3) | copy-done | bytes 131096
  9.6 0.7 copy-done.4
  10.2 0.4 shard_map.85
  10.7 0.0 collective-permute-done
  10.7 0.0 collective-permute-done.1
  10.7 0.0 collective-permute-done.2
  10.7 0.3 shard_map.86
  11.0 2.5 %collective-permute-start.3 = (bf16[16,2048]{1,0:T(8,128)(2,1)S(1)}, bf16[16,2048]{1,0:T(8,128)(2,1)S(1)}, u32[]{:S(2)}, u32[]{:S(2)}) collective-permute-start(bf16[16,2048]{1,0:T(8,128)(2,1)S(1)} %get-tuple-element.52), channel_id=1, source_target_pairs={{0,12},{4,0},{8,4},{12,8},{1,13},{5,1},{9,5},{13,9},{2,14},{6,2},{... | collective-permute-start | bytes 196616 | tf_op jit(solution)/shard_map/ppermute | solution.py:154
  13.5 0.6 collective-permute-start.5
  14.1 3.2 %collective-permute-start.6 = (bf16[16,2,3584]{2,0,1:T(8,128)(2,1)S(1)}, bf16[16,2,3584]{2,0,1:T(8,128)(2,1)S(1)}, u32[]{:S(2)}, u32[]{:S(2)}) collective-permute-start(bf16[16,2,3584]{2,0,1:T(8,128)(2,1)S(1)} %copy.11), channel_id=1, source_target_pairs={{0,12},{4,0},{8,4},{12,8},{1,13},{5,1},{9,5},{13,9},{2,14},{6,2},{... | collective-permute-start | bytes 688136 | tf_op jit(solution)/shard_map/ppermute | solution.py:154
  17.4 0.1 broadcast_in_dim.3
  17.5 0.1 reshape_reshape.3.row_holder
  17.5 2.5 %copy.16 = bf16[256,2,3584]{2,0,1:T(8,128)(2,1)S(1)} copy(bf16[256,2,3584]{2,1,0:T(2,128)(2,1)} %param.7) | data formatting | bytes 7340032 | tf_op jit(solution)/shard_map/optimization_barrier | solution.py:175
  20.1 1.2 %collective-permute-start.7 = (bf16[16,2,3584]{2,0,1:T(8,128)(2,1)S(1)}, bf16[16,2,3584]{2,0,1:T(8,128)(2,1)S(1)}, u32[]{:S(2)}, u32[]{:S(2)}) collective-permute-start(bf16[16,2,3584]{2,0,1:T(8,128)(2,1)S(1)} %copy.12), channel_id=1, source_target_pairs={{0,8},{4,12},{8,0},{12,4},{1,9},{5,13},{9,1},{13,5},{2,10},{6,14},... | collective-permute-start | bytes 688136 | tf_op jit(solution)/shard_map/ppermute | solution.py:154
  21.3 2.3 %shard_map.87 = (bf16[256,3584]{1,0:T(8,128)(2,1)S(1)}, bf16[256,3584]{1,0:T(8,128)(2,1)S(1)}) custom-call(bf16[2,256,3584]{2,1,0:T(8,128)(2,1)S(1)} %bitcast.13, bf16[256,3584]{1,0:T(8,128)(2,1)S(1)} %copy-done.1), custom_call_target="tpu_custom_call" | custom-call | flops 1 | bytes 1 | tf_op jit(solution)/shard_map/pallas_call | solution.py:185
  23.7 0.0 collective-permute-done.3.refs_1_
  23.7 0.1 collective-permute-start.8
  23.8 0.5 shard_map.92
  24.2 0.1 collective-permute-start.14
  24.3 1.2 %collective-permute-done.14 = f32[16,256]{1,0:T(8,128)S(1)} collective-permute-done((f32[16,256]{1,0:T(8,128)S(1)}, f32[16,256]{1,0:T(8,128)S(1)}, u32[]{:S(2)}, u32[]{:S(2)}) %collective-permute-start.14) | collective-permute-done | bytes 16416 | tf_op jit(solution)/shard_map/ppermute | solution.py:201
  25.5 1.5 %collective-permute-start.15 = (f32[16,256]{1,0:T(8,128)S(1)}, f32[16,256]{1,0:T(8,128)S(1)}, u32[]{:S(2)}, u32[]{:S(2)}) collective-permute-start(f32[16,256]{1,0:T(8,128)S(1)} %add.8.low), channel_id=1, source_target_pairs={{0,2},{2,0},{1,3},{3,1},{4,6},{6,4},{5,7},{7,5},{8,10},{10,8},{9,1... | collective-permute-start | bytes 49160 | tf_op jit(solution)/shard_map/ppermute | solution.py:201
  27.0 2.2 %collective-permute-done.15.more = f32[16,256]{1,0:T(8,128)S(1)} collective-permute-done((f32[16,256]{1,0:T(8,128)S(1)}, f32[16,256]{1,0:T(8,128)S(1)}, u32[]{:S(2)}, u32[]{:S(2)}) %collective-permute-start.15) | collective-permute-done | bytes 16416 | tf_op jit(solution)/shard_map/ppermute | solution.py:201
  29.2 0.8 %shard_map.93 = (bf16[2,16,3584]{2,1,0:T(8,128)(2,1)S(1)}, bf16[2,16,3584]{2,1,0:T(8,128)(2,1)S(1)}, bf16[2,16,3584]{2,1,0:T(8,128)(2,1)S(1)}, bf16[2,16,3584]{2,1,0:T(8,128)(2,1)S(1)}) custom-call(s32[1,256]{1,0:T(1,128)S(1)} %reshape_reshape.3.row_holder, f32[16,256]{1,0:T(8,128)S(1)} %add.8.low, f32[16,256]{1,0:T(8,128)S(1)} %collective-permute-done.15.more, ...), custom_call_target="tpu_custom_call" | custom-call | flops 1 | bytes 1 | tf_op jit(solution)/shard_map/pallas_call | solution.py:215
  30.0 2.4 %collective-permute-start.16 = (bf16[2,16,3584]{2,1,0:T(8,128)(2,1)S(1)}, bf16[2,16,3584]{2,1,0:T(8,128)(2,1)S(1)}, u32[]{:S(2)}, u32[]{:S(2)}) collective-permute-start(bf16[2,16,3584]{2,1,0:T(8,128)(2,1)S(1)} %get-tuple-element.74), channel_id=1, source_target_pairs={{0,4},{4,8},{8,12},{12,0},{1,5},{5,9},{9,13},{13,1},{2,6},{6,10},{... | collective-permute-start | bytes 688136 | tf_op jit(solution)/shard_map/ppermute | solution.py:154
  32.4 2.6 %collective-permute-start.17 = (bf16[2,16,3584]{2,1,0:T(8,128)(2,1)S(1)}, bf16[2,16,3584]{2,1,0:T(8,128)(2,1)S(1)}, u32[]{:S(2)}, u32[]{:S(2)}) collective-permute-start(bf16[2,16,3584]{2,1,0:T(8,128)(2,1)S(1)} %get-tuple-element.75), channel_id=1, source_target_pairs={{0,8},{4,12},{8,0},{12,4},{1,9},{5,13},{9,1},{13,5},{2,10},{6,14},... | collective-permute-start | bytes 688136 | tf_op jit(solution)/shard_map/ppermute | solution.py:154
  35.0 0.0 collective-permute-done.6
  35.0 2.8 %collective-permute-start.18 = (bf16[2,16,3584]{2,1,0:T(8,128)(2,1)S(1)}, bf16[2,16,3584]{2,1,0:T(8,128)(2,1)S(1)}, u32[]{:S(2)}, u32[]{:S(2)}) collective-permute-start(bf16[2,16,3584]{2,1,0:T(8,128)(2,1)S(1)} %get-tuple-element.76), channel_id=1, source_target_pairs={{0,12},{4,0},{8,4},{12,8},{1,13},{5,1},{9,5},{13,9},{2,14},{6,2},{... | collective-permute-start | bytes 688136 | tf_op jit(solution)/shard_map/ppermute | solution.py:154
  37.9 12.1 %collective-permute-done.7 = bf16[16,2,3584]{2,0,1:T(8,128)(2,1)S(1)} collective-permute-done((bf16[16,2,3584]{2,0,1:T(8,128)(2,1)S(1)}, bf16[16,2,3584]{2,0,1:T(8,128)(2,1)S(1)}, u32[]{:S(2)}, u32[]{:S(2)}) %collective-permute-start.7) | collective-permute-done | bytes 229408 | tf_op jit(solution)/shard_map/ppermute | solution.py:154
  49.9 1.2 %shard_map.88 = f32[16,256]{1,0:T(8,128)S(1)} custom-call(s32[1,256]{1,0:T(1,128)S(1)} %reshape_reshape.3.row_holder, bf16[256,3584]{1,0:T(8,128)(2,1)S(1)} %get-tuple-element.59.gate, bf16[256,3584]{1,0:T(8,128)(2,1)S(1)} %get-tuple-element.60.up, bf16[2,16,3584]{2,1,0:T(8,128)(2,1)S(1)} %bitcast.14, bf16[2,16,3584]{2,1,0:T(8,128)(2,1)S(1)} %bitcast.15, ...), custom_call_target="tpu_custom_call" | custom-call | flops 1 | bytes 1 | tf_op jit(solution)/shard_map/pallas_call | solution.py:221
  51.2 0.1 collective-permute-start.9
  51.2 1.2 %collective-permute-done.9 = f32[16,256]{1,0:T(8,128)S(1)} collective-permute-done((f32[16,256]{1,0:T(8,128)S(1)}, f32[16,256]{1,0:T(8,128)S(1)}, u32[]{:S(2)}, u32[]{:S(2)}) %collective-permute-start.9) | collective-permute-done | bytes 16416 | tf_op jit(solution)/shard_map/ppermute | solution.py:201
  52.4 1.5 %collective-permute-start.10 = (f32[16,256]{1,0:T(8,128)S(1)}, f32[16,256]{1,0:T(8,128)S(1)}, u32[]{:S(2)}, u32[]{:S(2)}) collective-permute-start(f32[16,256]{1,0:T(8,128)S(1)} %add.7.low), channel_id=1, source_target_pairs={{0,2},{2,0},{1,3},{3,1},{4,6},{6,4},{5,7},{7,5},{8,10},{10,8},{9,1... | collective-permute-start | bytes 49160 | tf_op jit(solution)/shard_map/ppermute | solution.py:201
  53.9 2.2 %collective-permute-done.10.more = f32[16,256]{1,0:T(8,128)S(1)} collective-permute-done((f32[16,256]{1,0:T(8,128)S(1)}, f32[16,256]{1,0:T(8,128)S(1)}, u32[]{:S(2)}, u32[]{:S(2)}) %collective-permute-start.10) | collective-permute-done | bytes 16416 | tf_op jit(solution)/shard_map/ppermute | solution.py:201
  56.2 0.3 shard_map.90
  56.5 0.1 collective-permute-start.11
  56.5 0.1 collective-permute-start.12
  56.6 0.0 collective-permute-done.16.refs_5_
  56.6 3.7 %collective-permute-start.13 = (bf16[16,2048]{1,0:T(8,128)(2,1)S(1)}, bf16[16,2048]{1,0:T(8,128)(2,1)S(1)}, u32[]{:S(2)}, u32[]{:S(2)}) collective-permute-start(bf16[16,2048]{1,0:T(8,128)(2,1)S(1)} %get-tuple-element.72), channel_id=1, source_target_pairs={{0,12},{4,0},{8,4},{12,8},{1,13},{5,1},{9,5},{13,9},{2,14},{6,2},{... | collective-permute-start | bytes 196616 | tf_op jit(solution)/shard_map/ppermute | solution.py:154
  60.3 1.4 %shard_map.89 = bf16[256,2048]{1,0:T(8,128)(2,1)} custom-call(s32[1,256]{1,0:T(1,128)S(1)} %reshape_reshape.3.row_holder, f32[16,256]{1,0:T(8,128)S(1)} %add.7.low, f32[16,256]{1,0:T(8,128)S(1)} %collective-permute-done.10.more, bf16[16,2048]{1,0:T(8,128)(2,1)S(1)} %get-tuple-element.65.refs_0_, bf16[16,2048]{1,0:T(8,128)(2,1)S(1)} %collective-permute-done.3.refs_1_, ...), custom_call_target="tpu_custom_call" | custom-call | flops 1 | bytes 1 | tf_op jit(solution)/shard_map/pallas_call | solution.py:232
  61.8 1.7 %shard_map.94 = f32[2,16,2,3584]{3,2,1,0:T(2,128)} custom-call(s32[1,8]{1,0:T(1,128)S(1)} %get-tuple-element.40.refs_0_, s32[1,8]{1,0:T(1,128)S(1)} %bitcast.19, s32[1,8]{1,0:T(1,128)S(1)} %bitcast.22, s32[1,8]{1,0:T(1,128)S(1)} %bitcast.25, bf16[2,16,3584]{2,1,0:T(8,128)(2,1)S(1)} %get-tuple-element.73.refs_4_, ...), custom_call_target="tpu_custom_call" | custom-call | flops 1 | bytes 1 | tf_op jit(solution)/shard_map/pallas_call | solution.py:244
  63.5 0.0 collective-permute-done.11.refs_5_
  63.5 0.9 %collective-permute-done.12.refs_6_ = bf16[16,2048]{1,0:T(8,128)(2,1)S(1)} collective-permute-done((bf16[16,2048]{1,0:T(8,128)(2,1)S(1)}, bf16[16,2048]{1,0:T(8,128)(2,1)S(1)}, u32[]{:S(2)}, u32[]{:S(2)}) %collective-permute-start.12) | collective-permute-done | bytes 65568 | tf_op jit(solution)/shard_map/ppermute | solution.py:154
  64.4 0.0 collective-permute-done.13.refs_7_
  64.4 1.0 %shard_map.91 = f32[2,16,2048]{2,1,0:T(8,128)} custom-call(s32[1,8]{1,0:T(1,128)S(1)} %get-tuple-element.40.refs_0_, s32[1,8]{1,0:T(1,128)S(1)} %bitcast.20, s32[1,8]{1,0:T(1,128)S(1)} %bitcast.23, s32[1,8]{1,0:T(1,128)S(1)} %bitcast.26, bf16[16,2048]{1,0:T(8,128)(2,1)S(1)} %get-tuple-element.69.refs_4_, ...), custom_call_target="tpu_custom_call" | custom-call | flops 1 | bytes 1 | tf_op jit(solution)/shard_map/pallas_call | solution.py:248
  (20 shorter events, 0.1 us)
Async XLA Ops:
  0.6 10.1 %collective-permute-start = (s32[8]{0:T(128)}, s32[8]{0:T(128)S(1)}, u32[]{:S(2)}, u32[]{:S(2)}) collective-permute-start(s32[8]{0:T(128)} %param.11), channel_id=1, source_target_pairs={{0,4},{4,8},{8,12},{12,0},{1,5},{5,9},{9,13},{13,1},{2,6},{6,10},{... | collective-permute-start | bytes 104 | tf_op jit(solution)/shard_map/ppermute | solution.py:154
  3.7 7.0 %collective-permute-start.1 = (s32[8]{0:T(128)}, s32[8]{0:T(128)S(1)}, u32[]{:S(2)}, u32[]{:S(2)}) collective-permute-start(s32[8]{0:T(128)} %param.11), channel_id=1, source_target_pairs={{0,8},{4,12},{8,0},{12,4},{1,9},{5,13},{9,1},{13,5},{2,10},{6,14},... | collective-permute-start | bytes 104 | tf_op jit(solution)/shard_map/ppermute | solution.py:154
  6.3 4.4 %collective-permute-start.2 = (s32[8]{0:T(128)}, s32[8]{0:T(128)S(1)}, u32[]{:S(2)}, u32[]{:S(2)}) collective-permute-start(s32[8]{0:T(128)} %param.11), channel_id=1, source_target_pairs={{0,12},{4,0},{8,4},{12,8},{1,13},{5,1},{9,5},{13,9},{2,14},{6,2},{... | collective-permute-start | bytes 104 | tf_op jit(solution)/shard_map/ppermute | solution.py:154
  7.6 1.0 %copy-start.2 = (bf16[2,16,2,3584]{3,2,1,0:T(2,128)(2,1)S(1)}, bf16[2,16,2,3584]{3,2,1,0:T(2,128)(2,1)}, u32[]{:S(2)}) copy-start(bf16[2,16,2,3584]{3,2,1,0:T(2,128)(2,1)} %up.1) | copy-start | bytes 1376260
  8.7 0.9 %copy-start.3 = (bf16[2,16,2048]{2,1,0:T(8,128)(2,1)S(1)}, bf16[2,16,2048]{2,1,0:T(8,128)(2,1)}, u32[]{:S(2)}) copy-start(bf16[2,16,2048]{2,1,0:T(8,128)(2,1)} %down.1) | copy-start | bytes 393220
  9.6 0.7 %copy-start.4 = (s32[8]{0:T(128)S(1)}, s32[8]{0:T(128)}, u32[]{:S(2)}) copy-start(s32[8]{0:T(128)} %param.11) | copy-start | bytes 100
  11.0 12.7 %collective-permute-start.3 = (bf16[16,2048]{1,0:T(8,128)(2,1)S(1)}, bf16[16,2048]{1,0:T(8,128)(2,1)S(1)}, u32[]{:S(2)}, u32[]{:S(2)}) collective-permute-start(bf16[16,2048]{1,0:T(8,128)(2,1)S(1)} %get-tuple-element.52), channel_id=1, source_target_pairs={{0,12},{4,0},{8,4},{12,8},{1,13},{5,1},{9,5},{13,9},{2,14},{6,2},{... | collective-permute-start | bytes 196616 | tf_op jit(solution)/shard_map/ppermute | solution.py:154
  13.5 10.3 %collective-permute-start.4 = (bf16[16,2048]{1,0:T(8,128)(2,1)S(1)}, bf16[16,2048]{1,0:T(8,128)(2,1)S(1)}, u32[]{:S(2)}, u32[]{:S(2)}) collective-permute-start(bf16[16,2048]{1,0:T(8,128)(2,1)S(1)} %get-tuple-element.53), channel_id=1, source_target_pairs={{0,8},{4,12},{8,0},{12,4},{1,9},{5,13},{9,1},{13,5},{2,10},{6,14},... | collective-permute-start | bytes 196616 | tf_op jit(solution)/shard_map/ppermute | solution.py:154
  13.5 10.3 %collective-permute-start.5 = (bf16[16,2048]{1,0:T(8,128)(2,1)S(1)}, bf16[16,2048]{1,0:T(8,128)(2,1)S(1)}, u32[]{:S(2)}, u32[]{:S(2)}) collective-permute-start(bf16[16,2048]{1,0:T(8,128)(2,1)S(1)} %get-tuple-element.54), channel_id=1, source_target_pairs={{0,4},{4,8},{8,12},{12,0},{1,5},{5,9},{9,13},{13,1},{2,6},{6,10},{... | collective-permute-start | bytes 196616 | tf_op jit(solution)/shard_map/ppermute | solution.py:154
  14.1 20.8 %collective-permute-start.6 = (bf16[16,2,3584]{2,0,1:T(8,128)(2,1)S(1)}, bf16[16,2,3584]{2,0,1:T(8,128)(2,1)S(1)}, u32[]{:S(2)}, u32[]{:S(2)}) collective-permute-start(bf16[16,2,3584]{2,0,1:T(8,128)(2,1)S(1)} %copy.11), channel_id=1, source_target_pairs={{0,12},{4,0},{8,4},{12,8},{1,13},{5,1},{9,5},{13,9},{2,14},{6,2},{... | collective-permute-start | bytes 688136 | tf_op jit(solution)/shard_map/ppermute | solution.py:154
  17.5 3.8 %copy-start.1 = (bf16[256,3584]{1,0:T(8,128)(2,1)S(1)}, bf16[256,3584]{1,0:T(8,128)(2,1)}, u32[]{:S(2)}) copy-start(bf16[256,3584]{1,0:T(8,128)(2,1)} %hidden) | copy-start | bytes 5505028
  20.1 29.8 %collective-permute-start.7 = (bf16[16,2,3584]{2,0,1:T(8,128)(2,1)S(1)}, bf16[16,2,3584]{2,0,1:T(8,128)(2,1)S(1)}, u32[]{:S(2)}, u32[]{:S(2)}) collective-permute-start(bf16[16,2,3584]{2,0,1:T(8,128)(2,1)S(1)} %copy.12), channel_id=1, source_target_pairs={{0,8},{4,12},{8,0},{12,4},{1,9},{5,13},{9,1},{13,5},{2,10},{6,14},... | collective-permute-start | bytes 688136 | tf_op jit(solution)/shard_map/ppermute | solution.py:154
  21.3 2.5 %copy-start = (bf16[256,2048]{1,0:T(8,128)(2,1)S(1)}, bf16[256,2048]{1,0:T(8,128)(2,1)}, u32[]{:S(2)}) copy-start(bf16[256,2048]{1,0:T(8,128)(2,1)} %acts.3) | copy-start | bytes 3145732
  23.7 26.3 %collective-permute-start.8 = (bf16[16,2,3584]{2,0,1:T(8,128)(2,1)S(1)}, bf16[16,2,3584]{2,0,1:T(8,128)(2,1)S(1)}, u32[]{:S(2)}, u32[]{:S(2)}) collective-permute-start(bf16[16,2,3584]{2,0,1:T(8,128)(2,1)S(1)} %copy.13), channel_id=1, source_target_pairs={{0,4},{4,8},{8,12},{12,0},{1,5},{5,9},{9,13},{13,1},{2,6},{6,10},{... | collective-permute-start | bytes 688136 | tf_op jit(solution)/shard_map/ppermute | solution.py:154
  24.2 1.2 %collective-permute-start.14 = (f32[16,256]{1,0:T(8,128)S(1)}, f32[16,256]{1,0:T(8,128)S(1)}, u32[]{:S(2)}, u32[]{:S(2)}) collective-permute-start(f32[16,256]{1,0:T(8,128)S(1)} %shard_map.92), channel_id=1, source_target_pairs={{0,1},{1,0},{2,3},{3,2},{4,5},{5,4},{6,7},{7,6},{8,9},{9,8},{10,11... | collective-permute-start | bytes 49160 | tf_op jit(solution)/shard_map/ppermute | solution.py:201
  25.5 3.7 %collective-permute-start.15 = (f32[16,256]{1,0:T(8,128)S(1)}, f32[16,256]{1,0:T(8,128)S(1)}, u32[]{:S(2)}, u32[]{:S(2)}) collective-permute-start(f32[16,256]{1,0:T(8,128)S(1)} %add.8.low), channel_id=1, source_target_pairs={{0,2},{2,0},{1,3},{3,1},{4,6},{6,4},{5,7},{7,5},{8,10},{10,8},{9,1... | collective-permute-start | bytes 49160 | tf_op jit(solution)/shard_map/ppermute | solution.py:201
  30.0 26.6 %collective-permute-start.16 = (bf16[2,16,3584]{2,1,0:T(8,128)(2,1)S(1)}, bf16[2,16,3584]{2,1,0:T(8,128)(2,1)S(1)}, u32[]{:S(2)}, u32[]{:S(2)}) collective-permute-start(bf16[2,16,3584]{2,1,0:T(8,128)(2,1)S(1)} %get-tuple-element.74), channel_id=1, source_target_pairs={{0,4},{4,8},{8,12},{12,0},{1,5},{5,9},{9,13},{13,1},{2,6},{6,10},{... | collective-permute-start | bytes 688136 | tf_op jit(solution)/shard_map/ppermute | solution.py:154
  32.4 29.4 %collective-permute-start.17 = (bf16[2,16,3584]{2,1,0:T(8,128)(2,1)S(1)}, bf16[2,16,3584]{2,1,0:T(8,128)(2,1)S(1)}, u32[]{:S(2)}, u32[]{:S(2)}) collective-permute-start(bf16[2,16,3584]{2,1,0:T(8,128)(2,1)S(1)} %get-tuple-element.75), channel_id=1, source_target_pairs={{0,8},{4,12},{8,0},{12,4},{1,9},{5,13},{9,1},{13,5},{2,10},{6,14},... | collective-permute-start | bytes 688136 | tf_op jit(solution)/shard_map/ppermute | solution.py:154
  35.0 26.8 %collective-permute-start.18 = (bf16[2,16,3584]{2,1,0:T(8,128)(2,1)S(1)}, bf16[2,16,3584]{2,1,0:T(8,128)(2,1)S(1)}, u32[]{:S(2)}, u32[]{:S(2)}) collective-permute-start(bf16[2,16,3584]{2,1,0:T(8,128)(2,1)S(1)} %get-tuple-element.76), channel_id=1, source_target_pairs={{0,12},{4,0},{8,4},{12,8},{1,13},{5,1},{9,5},{13,9},{2,14},{6,2},{... | collective-permute-start | bytes 688136 | tf_op jit(solution)/shard_map/ppermute | solution.py:154
  51.2 1.2 %collective-permute-start.9 = (f32[16,256]{1,0:T(8,128)S(1)}, f32[16,256]{1,0:T(8,128)S(1)}, u32[]{:S(2)}, u32[]{:S(2)}) collective-permute-start(f32[16,256]{1,0:T(8,128)S(1)} %shard_map.88), channel_id=1, source_target_pairs={{0,1},{1,0},{2,3},{3,2},{4,5},{5,4},{6,7},{7,6},{8,9},{9,8},{10,11... | collective-permute-start | bytes 49160 | tf_op jit(solution)/shard_map/ppermute | solution.py:201
  52.4 3.7 %collective-permute-start.10 = (f32[16,256]{1,0:T(8,128)S(1)}, f32[16,256]{1,0:T(8,128)S(1)}, u32[]{:S(2)}, u32[]{:S(2)}) collective-permute-start(f32[16,256]{1,0:T(8,128)S(1)} %add.7.low), channel_id=1, source_target_pairs={{0,2},{2,0},{1,3},{3,1},{4,6},{6,4},{5,7},{7,5},{8,10},{10,8},{9,1... | collective-permute-start | bytes 49160 | tf_op jit(solution)/shard_map/ppermute | solution.py:201
  56.5 7.0 %collective-permute-start.11 = (bf16[16,2048]{1,0:T(8,128)(2,1)S(1)}, bf16[16,2048]{1,0:T(8,128)(2,1)S(1)}, u32[]{:S(2)}, u32[]{:S(2)}) collective-permute-start(bf16[16,2048]{1,0:T(8,128)(2,1)S(1)} %get-tuple-element.70), channel_id=1, source_target_pairs={{0,4},{4,8},{8,12},{12,0},{1,5},{5,9},{9,13},{13,1},{2,6},{6,10},{... | collective-permute-start | bytes 196616 | tf_op jit(solution)/shard_map/ppermute | solution.py:154
  56.5 7.8 %collective-permute-start.12 = (bf16[16,2048]{1,0:T(8,128)(2,1)S(1)}, bf16[16,2048]{1,0:T(8,128)(2,1)S(1)}, u32[]{:S(2)}, u32[]{:S(2)}) collective-permute-start(bf16[16,2048]{1,0:T(8,128)(2,1)S(1)} %get-tuple-element.71), channel_id=1, source_target_pairs={{0,8},{4,12},{8,0},{12,4},{1,9},{5,13},{9,1},{13,5},{2,10},{6,14},... | collective-permute-start | bytes 196616 | tf_op jit(solution)/shard_map/ppermute | solution.py:154
  56.6 7.7 %collective-permute-start.13 = (bf16[16,2048]{1,0:T(8,128)(2,1)S(1)}, bf16[16,2048]{1,0:T(8,128)(2,1)S(1)}, u32[]{:S(2)}, u32[]{:S(2)}) collective-permute-start(bf16[16,2048]{1,0:T(8,128)(2,1)S(1)} %get-tuple-element.72), channel_id=1, source_target_pairs={{0,12},{4,0},{8,4},{12,8},{1,13},{5,1},{9,5},{13,9},{2,14},{6,2},{... | collective-permute-start | bytes 196616 | tf_op jit(solution)/shard_map/ppermute | solution.py:154

commit v3 on v2

--- a/solution.py
+++ b/solution.py
@@ -28,13 +28,18 @@
     )
 
 
+def steps(count):
+    return enumerate(range(count - 1, -1, -1))
+
+
 def asked_slot(ids, slots):
     me = lax.axis_index("tenant")
     return jnp.max(jnp.where(lax.div(ids, slots) == me, lax.rem(ids, slots), 0))
 
 
 def peer_index(k, count):
-    return lax.rem(lax.axis_index("tenant") + k, count)
+    me = lax.axis_index("tenant")
+    return me ^ k if count & (count - 1) == 0 else lax.rem(me + k, count)
 
 
 def bring(ids, down, up, ids_out, down_out, up_out, arrived):
@@ -58,17 +63,17 @@
 def choose(count, slots, *refs):
     ids, down, up = refs[:count], refs[count], refs[count + 1]
     outs = refs[count + 2 :]
-    for k in range(count):
-        asked = asked_slot(ids[k][...], slots)
-        outs[k][...] = down[asked]
-        outs[count + k][...] = up[asked]
+    for i in range(count):
+        asked = asked_slot(ids[i][...], slots)
+        outs[i][...] = down[asked]
+        outs[count + i][...] = up[asked]
 
 
 def keep_own(full, row_holder, count, rank):
     total = jnp.zeros((rank, full.shape[1]), F32)
-    for k in range(count):
+    for i, k in steps(count):
         own = row_holder == peer_index(k, count)
-        total = total + jnp.where(own, full[k * rank : (k + 1) * rank], 0.0)
+        total = total + jnp.where(own, full[i * rank : (i + 1) * rank], 0.0)
     return total
 
 
@@ -90,9 +95,9 @@
 
 def fill_wide(wide, row_holder, low, count, rank):
     narrow = low.astype(BF).astype(F32)
-    for k in range(count):
+    for i, k in steps(count):
         own = row_holder == peer_index(k, count)
-        wide[pl.ds(k * rank, rank), :] = jnp.where(own, narrow, 0.0).astype(BF)
+        wide[pl.ds(i * rank, rank), :] = jnp.where(own, narrow, 0.0).astype(BF)
 
 
 def parts_b(count, rank, row_holder, low, more, gate, up, *refs):
@@ -147,18 +152,19 @@
     units = up.shape[3]
     rows = acts.shape[0]
     block_rows = rows // ids.shape[0]
-    every = range(T)
     shape = jax.ShapeDtypeStruct
 
     def shift(x, k):
+        if T & (T - 1) == 0:
+            return lax.ppermute(x, "tenant", [(i, i ^ abs(k)) for i in range(T)])
         return lax.ppermute(x, "tenant", [(i, (i + k) % T) for i in range(T)])
 
-    order = sorted(range(1, T), key=lambda k: -min(k, T - k))
+    order = list(range(T - 1, 0, -1))
 
     ids_from = {0: ids}
     for k in order:
         ids_from[k] = shift(ids, k)
-    ids_from = [ids_from[k].reshape(1, -1) for k in every]
+    ids_from = [ids_from[k].reshape(1, -1) for k in order + [0]]
 
     own_ids = ids.reshape(1, -1)
     own_ids, own_down, own_up = on_chip(
@@ -167,19 +173,19 @@
         [pltpu.SemaphoreType.DMA((3,))],
         in_specs=[pl.BlockSpec(memory_space=pl.ANY)] * 3,
     )(own_ids, down, up)
-    ids_from[0] = own_ids
+    ids_from[-1] = own_ids
     sends = on_chip(
         functools.partial(choose, T, slots),
         [shape((rank, width), BF)] * T + [shape((rank, 2, units), BF)] * T,
     )(*ids_from, own_down, own_up)
     sends, saved, hidden = lax.optimization_barrier((sends, saved, hidden))
-    down_from, up_from = {0: sends[0]}, {0: sends[T]}
-    for k in order:
-        down_from[k] = shift(sends[k], -k)
-    for k in order:
-        up_from[k] = shift(sends[T + k], -k)
-    down_from = [down_from[k] for k in every]
-    up_from = [jnp.swapaxes(up_from[k], 0, 1) for k in every]
+    down_from, up_from = {0: sends[T - 1]}, {0: sends[2 * T - 1]}
+    for k in order:
+        down_from[k] = shift(sends[T - 1 - k], -k)
+    for k in order:
+        up_from[k] = shift(sends[2 * T - 1 - k], -k)
+    down_from = [down_from[k] for k in order + [0]]
+    up_from = [jnp.swapaxes(up_from[k], 0, 1) for k in order + [0]]
 
     saved_by_gate = jnp.swapaxes(saved, 0, 1)
     grad_gate, grad_up = on_chip(
@@ -235,20 +241,20 @@
         [pltpu.VMEM((T * rank, width), BF), pltpu.VMEM((T * rank, rows), BF)],
     )(row_holder, low_out, more_out, *down_from)
 
-    got_b = {0: back_b[0]}
-    for k in order:
-        got_b[k] = shift(back_b[k], k)
-    got_a = {0: back_a[0]}
-    for k in order:
-        got_a[k] = shift(back_a[k], k)
+    got_b = {0: back_b[T - 1]}
+    for k in order:
+        got_b[k] = shift(back_b[T - 1 - k], k)
+    got_a = {0: back_a[T - 1]}
+    for k in order:
+        got_a[k] = shift(back_a[T - 1 - k], k)
     grad_b = on_chip(
         part(held_sum_b, T, slots),
         shape((slots, rank, 2, units), F32),
-    )(*ids_from, *[got_b[k] for k in every])
+    )(*ids_from, *[got_b[k] for k in order + [0]])
     grad_a = on_chip(
         part(held_sum_a, T, slots),
         shape((slots, rank, width), F32),
-    )(*ids_from, *[got_a[k] for k in every])
+    )(*ids_from, *[got_a[k] for k in order + [0]])
     return grad_acts, grad_a, grad_b
 
 

time: 65.6 us -> 64.8 us (0.988)
  starting transfers between devices: 29.4 us -> 26.8 us
  waiting for transfers between devices: 19.8 us -> 21.7 us
    ppermute x15, starting transfers between devices: 26.3 us -> 23.7 us  [shift(): return lax.ppermute(x, 'tenant', [(i, i ^ abs(k)) for i in range(T)])]
    ppermute x15, waiting for transfers between devices: 13 us -> 14.9 us  [shift(): return lax.ppermute(x, 'tenant', [(i, i ^ abs(k)) for i in range(T)])]
  transfers between devices with their start and end apart: 19 -> 19, of which waited for: 6 -> 8; matrix products, arithmetic and copies ran while one was open for 4% -> 4% of each run, Pallas kernels for 13% -> 13%
where the time goes in v3:
time: 64.8 us; the launch traced here: 64.6 us
  starting transfers between devices  26.8 us (41%)
  waiting for transfers between devices  21.7 us (33%)
  Pallas kernels  9.93 us (15%)
  local copies, waits for them, and re-layouts  5.37 us (8%)
  between operations  0.78 us (1%)
    ppermute x15, starting transfers between devices, shift(): return lax.ppermute(x, 'tenant', [(i, i ^ abs(k)) for i in range(T)])  23.7 us
    ppermute x15, waiting for transfers between devices, shift(): return lax.ppermute(x, 'tenant', [(i, i ^ abs(k)) for i in range(T)])  14.9 us
    ppermute x4, waiting for transfers between devices, feature_sum(): lax.ppermute(x, axis, [(i, (i + k) % n) for i in range(n)])  6.85 us
    ppermute x4, starting transfers between devices, feature_sum(): lax.ppermute(x, axis, [(i, (i + k) % n) for i in range(n)])  3.11 us
    optimization_barrier x5, local copies, waits for them, and re-layouts, on_device(): sends, saved, hidden = lax.optimization_barrier((sends, saved, hidden))  2.63 us
    unnamed x10, local copies, waits for them, and re-layouts  2.59 us
    pallas_call x1, Pallas kernels, on_device(): on_chip(gated_grad, [shape((rows, units), BF)] * 2, grid=(8,), in_specs=[...  2.33 us
    pallas_call x1, Pallas kernels, on_device(): on_chip(part(held_sum_b, T, slots), shape((slots, rank, 2, units), F32))  1.7 us
  transfers between devices with their start and end apart: 19, of which 8 were waited for; matrix products, arithmetic and copies ran while one was open for 4% of the time, Pallas kernels for 13%

profile of v3, /device:TPU:0, one launch (start us, length us, event | category | flops | bytes accessed | tf_op | source)
XLA Modules:
  0.0 64.6 jit_solution(4611042397245363381)
XLA Ops:
  0.6 5.1 %collective-permute-start = (s32[8]{0:T(128)}, s32[8]{0:T(128)S(1)}, u32[]{:S(2)}, u32[]{:S(2)}) collective-permute-start(s32[8]{0:T(128)} %param.11), channel_id=1, source_target_pairs={{0,12},{4,8},{8,4},{12,0},{1,13},{5,9},{9,5},{13,1},{2,14},{6,10},... | collective-permute-start | bytes 104 | tf_op jit(solution)/shard_map/ppermute | solution.py:159
  5.7 0.6 collective-permute-start.2
  6.4 1.0 %copy-done.2 = bf16[2,16,2,3584]{3,2,1,0:T(2,128)(2,1)S(1)} copy-done((bf16[2,16,2,3584]{3,2,1,0:T(2,128)(2,1)S(1)}, bf16[2,16,2,3584]{3,2,1,0:T(2,128)(2,1)}, u32[]{:S(2)}) %copy-start.2) | copy-done | bytes 458776
  7.4 0.9 %copy-done.3 = bf16[2,16,2048]{2,1,0:T(8,128)(2,1)S(1)} copy-done((bf16[2,16,2048]{2,1,0:T(8,128)(2,1)S(1)}, bf16[2,16,2048]{2,1,0:T(8,128)(2,1)}, u32[]{:S(2)}) %copy-start.3) | copy-done | bytes 131096
  8.3 0.7 %copy-done.4 = s32[8]{0:T(128)S(1)} copy-done((s32[8]{0:T(128)S(1)}, s32[8]{0:T(128)}, u32[]{:S(2)}) %copy-start.4) | copy-done | bytes 56
  9.0 0.4 shard_map.85
  9.4 0.0 collective-permute-done
  9.4 0.9 %collective-permute-done.1 = s32[8]{0:T(128)S(1)} collective-permute-done((s32[8]{0:T(128)}, s32[8]{0:T(128)S(1)}, u32[]{:S(2)}, u32[]{:S(2)}) %collective-permute-start.1) | collective-permute-done | bytes 64 | tf_op jit(solution)/shard_map/ppermute | solution.py:159
  10.3 0.0 collective-permute-done.2
  10.3 0.3 shard_map.86
  10.6 2.9 %collective-permute-start.3 = (bf16[16,2048]{1,0:T(8,128)(2,1)S(1)}, bf16[16,2048]{1,0:T(8,128)(2,1)S(1)}, u32[]{:S(2)}, u32[]{:S(2)}) collective-permute-start(bf16[16,2048]{1,0:T(8,128)(2,1)S(1)} %get-tuple-element.51), channel_id=1, source_target_pairs={{0,12},{4,8},{8,4},{12,0},{1,13},{5,9},{9,5},{13,1},{2,14},{6,10},... | collective-permute-start | bytes 196616 | tf_op jit(solution)/shard_map/ppermute | solution.py:159
  13.6 0.0 collective-permute-start.4
  13.6 1.5 %collective-permute-start.5 = (bf16[16,2048]{1,0:T(8,128)(2,1)S(1)}, bf16[16,2048]{1,0:T(8,128)(2,1)S(1)}, u32[]{:S(2)}, u32[]{:S(2)}) collective-permute-start(bf16[16,2048]{1,0:T(8,128)(2,1)S(1)} %get-tuple-element.53), channel_id=1, source_target_pairs={{0,4},{4,0},{8,12},{12,8},{1,5},{5,1},{9,13},{13,9},{2,6},{6,2},{1... | collective-permute-start | bytes 196616 | tf_op jit(solution)/shard_map/ppermute | solution.py:159
  15.1 2.9 %collective-permute-start.6 = (bf16[16,2,3584]{2,0,1:T(8,128)(2,1)S(1)}, bf16[16,2,3584]{2,0,1:T(8,128)(2,1)S(1)}, u32[]{:S(2)}, u32[]{:S(2)}) collective-permute-start(bf16[16,2,3584]{2,0,1:T(8,128)(2,1)S(1)} %copy.10), channel_id=1, source_target_pairs={{0,12},{4,8},{8,4},{12,0},{1,13},{5,9},{9,5},{13,1},{2,14},{6,10},... | collective-permute-start | bytes 688136 | tf_op jit(solution)/shard_map/ppermute | solution.py:159
  18.1 0.1 broadcast_in_dim.3
  18.1 0.1 reshape_reshape.3.row_holder
  18.2 2.5 %copy.16 = bf16[256,2,3584]{2,0,1:T(8,128)(2,1)S(1)} copy(bf16[256,2,3584]{2,1,0:T(2,128)(2,1)} %param.7) | data formatting | bytes 7340032 | tf_op jit(solution)/shard_map/optimization_barrier | solution.py:181
  20.8 0.1 collective-permute-start.7
  20.9 0.0 copy-start
  20.9 2.3 %shard_map.87 = (bf16[256,3584]{1,0:T(8,128)(2,1)S(1)}, bf16[256,3584]{1,0:T(8,128)(2,1)S(1)}) custom-call(bf16[2,256,3584]{2,1,0:T(8,128)(2,1)S(1)} %bitcast.13, bf16[256,3584]{1,0:T(8,128)(2,1)S(1)} %copy-done.1), custom_call_target="tpu_custom_call" | custom-call | flops 1 | bytes 1 | tf_op jit(solution)/shard_map/pallas_call | solution.py:191
  23.3 1.5 %collective-permute-start.8 = (bf16[16,2,3584]{2,0,1:T(8,128)(2,1)S(1)}, bf16[16,2,3584]{2,0,1:T(8,128)(2,1)S(1)}, u32[]{:S(2)}, u32[]{:S(2)}) collective-permute-start(bf16[16,2,3584]{2,0,1:T(8,128)(2,1)S(1)} %copy.12), channel_id=1, source_target_pairs={{0,4},{4,0},{8,12},{12,8},{1,5},{5,1},{9,13},{13,9},{2,6},{6,2},{1... | collective-permute-start | bytes 688136 | tf_op jit(solution)/shard_map/ppermute | solution.py:159
  24.8 3.6 %collective-permute-done.4.refs_1_ = bf16[16,2048]{1,0:T(8,128)(2,1)S(1)} collective-permute-done((bf16[16,2048]{1,0:T(8,128)(2,1)S(1)}, bf16[16,2048]{1,0:T(8,128)(2,1)S(1)}, u32[]{:S(2)}, u32[]{:S(2)}) %collective-permute-start.4) | collective-permute-done | bytes 65568 | tf_op jit(solution)/shard_map/ppermute | solution.py:159
  28.4 0.4 shard_map.92
  28.9 0.1 collective-permute-start.14
  28.9 1.2 %collective-permute-done.14 = f32[16,256]{1,0:T(8,128)S(1)} collective-permute-done((f32[16,256]{1,0:T(8,128)S(1)}, f32[16,256]{1,0:T(8,128)S(1)}, u32[]{:S(2)}, u32[]{:S(2)}) %collective-permute-start.14) | collective-permute-done | bytes 16416 | tf_op jit(solution)/shard_map/ppermute | solution.py:207
  30.1 1.5 %collective-permute-start.15 = (f32[16,256]{1,0:T(8,128)S(1)}, f32[16,256]{1,0:T(8,128)S(1)}, u32[]{:S(2)}, u32[]{:S(2)}) collective-permute-start(f32[16,256]{1,0:T(8,128)S(1)} %add.8.low), channel_id=1, source_target_pairs={{0,2},{2,0},{1,3},{3,1},{4,6},{6,4},{5,7},{7,5},{8,10},{10,8},{9,1... | collective-permute-start | bytes 49160 | tf_op jit(solution)/shard_map/ppermute | solution.py:207
  31.6 2.2 %collective-permute-done.15.more = f32[16,256]{1,0:T(8,128)S(1)} collective-permute-done((f32[16,256]{1,0:T(8,128)S(1)}, f32[16,256]{1,0:T(8,128)S(1)}, u32[]{:S(2)}, u32[]{:S(2)}) %collective-permute-start.15) | collective-permute-done | bytes 16416 | tf_op jit(solution)/shard_map/ppermute | solution.py:207
  33.9 0.8 %shard_map.93 = (bf16[2,16,3584]{2,1,0:T(8,128)(2,1)S(1)}, bf16[2,16,3584]{2,1,0:T(8,128)(2,1)S(1)}, bf16[2,16,3584]{2,1,0:T(8,128)(2,1)S(1)}, bf16[2,16,3584]{2,1,0:T(8,128)(2,1)S(1)}) custom-call(s32[1,256]{1,0:T(1,128)S(1)} %reshape_reshape.3.row_holder, f32[16,256]{1,0:T(8,128)S(1)} %add.8.low, f32[16,256]{1,0:T(8,128)S(1)} %collective-permute-done.15.more, ...), custom_call_target="tpu_custom_call" | custom-call | flops 1 | bytes 1 | tf_op jit(solution)/shard_map/pallas_call | solution.py:221
  34.6 2.8 %collective-permute-start.16 = (bf16[2,16,3584]{2,1,0:T(8,128)(2,1)S(1)}, bf16[2,16,3584]{2,1,0:T(8,128)(2,1)S(1)}, u32[]{:S(2)}, u32[]{:S(2)}) collective-permute-start(bf16[2,16,3584]{2,1,0:T(8,128)(2,1)S(1)} %get-tuple-element.73), channel_id=1, source_target_pairs={{0,12},{4,8},{8,4},{12,0},{1,13},{5,9},{9,5},{13,1},{2,14},{6,10},... | collective-permute-start | bytes 688136 | tf_op jit(solution)/shard_map/ppermute | solution.py:159
  37.4 0.0 collective-permute-start.17
  37.4 0.0 collective-permute-done.6
  37.4 1.6 %collective-permute-start.18 = (bf16[2,16,3584]{2,1,0:T(8,128)(2,1)S(1)}, bf16[2,16,3584]{2,1,0:T(8,128)(2,1)S(1)}, u32[]{:S(2)}, u32[]{:S(2)}) collective-permute-start(bf16[2,16,3584]{2,1,0:T(8,128)(2,1)S(1)} %get-tuple-element.75), channel_id=1, source_target_pairs={{0,4},{4,0},{8,12},{12,8},{1,5},{5,1},{9,13},{13,9},{2,6},{6,2},{1... | collective-permute-start | bytes 688136 | tf_op jit(solution)/shard_map/ppermute | solution.py:159
  39.1 9.5 %collective-permute-done.7 = bf16[16,2,3584]{2,0,1:T(8,128)(2,1)S(1)} collective-permute-done((bf16[16,2,3584]{2,0,1:T(8,128)(2,1)S(1)}, bf16[16,2,3584]{2,0,1:T(8,128)(2,1)S(1)}, u32[]{:S(2)}, u32[]{:S(2)}) %collective-permute-start.7) | collective-permute-done | bytes 229408 | tf_op jit(solution)/shard_map/ppermute | solution.py:159
  48.6 0.0 collective-permute-done.8
  48.6 1.2 %shard_map.88 = f32[16,256]{1,0:T(8,128)S(1)} custom-call(s32[1,256]{1,0:T(1,128)S(1)} %reshape_reshape.3.row_holder, bf16[256,3584]{1,0:T(8,128)(2,1)S(1)} %get-tuple-element.59.gate, bf16[256,3584]{1,0:T(8,128)(2,1)S(1)} %get-tuple-element.60.up, bf16[2,16,3584]{2,1,0:T(8,128)(2,1)S(1)} %bitcast.15, bf16[2,16,3584]{2,1,0:T(8,128)(2,1)S(1)} %bitcast.16, ...), custom_call_target="tpu_custom_call" | custom-call | flops 1 | bytes 1 | tf_op jit(solution)/shard_map/pallas_call | solution.py:227
  49.9 0.1 collective-permute-start.9
  49.9 1.2 %collective-permute-done.9 = f32[16,256]{1,0:T(8,128)S(1)} collective-permute-done((f32[16,256]{1,0:T(8,128)S(1)}, f32[16,256]{1,0:T(8,128)S(1)}, u32[]{:S(2)}, u32[]{:S(2)}) %collective-permute-start.9) | collective-permute-done | bytes 16416 | tf_op jit(solution)/shard_map/ppermute | solution.py:207
  51.1 1.5 %collective-permute-start.10 = (f32[16,256]{1,0:T(8,128)S(1)}, f32[16,256]{1,0:T(8,128)S(1)}, u32[]{:S(2)}, u32[]{:S(2)}) collective-permute-start(f32[16,256]{1,0:T(8,128)S(1)} %add.7.low), channel_id=1, source_target_pairs={{0,2},{2,0},{1,3},{3,1},{4,6},{6,4},{5,7},{7,5},{8,10},{10,8},{9,1... | collective-permute-start | bytes 49160 | tf_op jit(solution)/shard_map/ppermute | solution.py:207
  52.6 2.3 %collective-permute-done.10.more = f32[16,256]{1,0:T(8,128)S(1)} collective-permute-done((f32[16,256]{1,0:T(8,128)S(1)}, f32[16,256]{1,0:T(8,128)S(1)}, u32[]{:S(2)}, u32[]{:S(2)}) %collective-permute-start.10) | collective-permute-done | bytes 16416 | tf_op jit(solution)/shard_map/ppermute | solution.py:207
  54.8 0.3 shard_map.90
  55.2 2.6 %collective-permute-start.11 = (bf16[16,2048]{1,0:T(8,128)(2,1)S(1)}, bf16[16,2048]{1,0:T(8,128)(2,1)S(1)}, u32[]{:S(2)}, u32[]{:S(2)}) collective-permute-start(bf16[16,2048]{1,0:T(8,128)(2,1)S(1)} %get-tuple-element.69), channel_id=1, source_target_pairs={{0,12},{4,8},{8,4},{12,0},{1,13},{5,9},{9,5},{13,1},{2,14},{6,10},... | collective-permute-start | bytes 196616 | tf_op jit(solution)/shard_map/ppermute | solution.py:159
  57.7 0.0 collective-permute-start.12
  57.7 0.0 collective-permute-done.16.refs_4_
  57.7 1.9 %collective-permute-start.13 = (bf16[16,2048]{1,0:T(8,128)(2,1)S(1)}, bf16[16,2048]{1,0:T(8,128)(2,1)S(1)}, u32[]{:S(2)}, u32[]{:S(2)}) collective-permute-start(bf16[16,2048]{1,0:T(8,128)(2,1)S(1)} %get-tuple-element.71), channel_id=1, source_target_pairs={{0,4},{4,0},{8,12},{12,8},{1,5},{5,1},{9,13},{13,9},{2,6},{6,2},{1... | collective-permute-start | bytes 196616 | tf_op jit(solution)/shard_map/ppermute | solution.py:159
  59.6 1.4 %shard_map.89 = bf16[256,2048]{1,0:T(8,128)(2,1)} custom-call(s32[1,256]{1,0:T(1,128)S(1)} %reshape_reshape.3.row_holder, f32[16,256]{1,0:T(8,128)S(1)} %add.7.low, f32[16,256]{1,0:T(8,128)S(1)} %collective-permute-done.10.more, bf16[16,2048]{1,0:T(8,128)(2,1)S(1)} %collective-permute-done.3.refs_0_, bf16[16,2048]{1,0:T(8,128)(2,1)S(1)} %collective-permute-done.4.refs_1_, ...), custom_call_target="tpu_custom_call" | custom-call | flops 1 | bytes 1 | tf_op jit(solution)/shard_map/pallas_call | solution.py:238
  61.1 1.7 %shard_map.94 = f32[2,16,2,3584]{3,2,1,0:T(2,128)} custom-call(s32[1,8]{1,0:T(1,128)S(1)} %bitcast.19, s32[1,8]{1,0:T(1,128)S(1)} %bitcast.22, s32[1,8]{1,0:T(1,128)S(1)} %bitcast.25, s32[1,8]{1,0:T(1,128)S(1)} %get-tuple-element.40.refs_3_, bf16[2,16,3584]{2,1,0:T(8,128)(2,1)S(1)} %collective-permute-done.16.refs_4_, ...), custom_call_target="tpu_custom_call" | custom-call | flops 1 | bytes 1 | tf_op jit(solution)/shard_map/pallas_call | solution.py:250
  62.8 0.8 %collective-permute-done.12.refs_5_ = bf16[16,2048]{1,0:T(8,128)(2,1)S(1)} collective-permute-done((bf16[16,2048]{1,0:T(8,128)(2,1)S(1)}, bf16[16,2048]{1,0:T(8,128)(2,1)S(1)}, u32[]{:S(2)}, u32[]{:S(2)}) %collective-permute-start.12) | collective-permute-done | bytes 65568 | tf_op jit(solution)/shard_map/ppermute | solution.py:159
  63.6 1.0 %shard_map.91 = f32[2,16,2048]{2,1,0:T(8,128)} custom-call(s32[1,8]{1,0:T(1,128)S(1)} %bitcast.20, s32[1,8]{1,0:T(1,128)S(1)} %bitcast.23, s32[1,8]{1,0:T(1,128)S(1)} %bitcast.26, s32[1,8]{1,0:T(1,128)S(1)} %get-tuple-element.40.refs_3_, bf16[16,2048]{1,0:T(8,128)(2,1)S(1)} %collective-permute-done.11.refs_4_, ...), custom_call_target="tpu_custom_call" | custom-call | flops 1 | bytes 1 | tf_op jit(solution)/shard_map/pallas_call | solution.py:254
  (20 shorter events, 0.1 us)
Async XLA Ops:
  0.6 8.8 %collective-permute-start = (s32[8]{0:T(128)}, s32[8]{0:T(128)S(1)}, u32[]{:S(2)}, u32[]{:S(2)}) collective-permute-start(s32[8]{0:T(128)} %param.11), channel_id=1, source_target_pairs={{0,12},{4,8},{8,4},{12,0},{1,13},{5,9},{9,5},{13,1},{2,14},{6,10},... | collective-permute-start | bytes 104 | tf_op jit(solution)/shard_map/ppermute | solution.py:159
  5.7 4.6 %collective-permute-start.1 = (s32[8]{0:T(128)}, s32[8]{0:T(128)S(1)}, u32[]{:S(2)}, u32[]{:S(2)}) collective-permute-start(s32[8]{0:T(128)} %param.11), channel_id=1, source_target_pairs={{0,8},{4,12},{8,0},{12,4},{1,9},{5,13},{9,1},{13,5},{2,10},{6,14},... | collective-permute-start | bytes 104 | tf_op jit(solution)/shard_map/ppermute | solution.py:159
  5.7 4.6 %collective-permute-start.2 = (s32[8]{0:T(128)}, s32[8]{0:T(128)S(1)}, u32[]{:S(2)}, u32[]{:S(2)}) collective-permute-start(s32[8]{0:T(128)} %param.11), channel_id=1, source_target_pairs={{0,4},{4,0},{8,12},{12,8},{1,5},{5,1},{9,13},{13,9},{2,6},{6,2},{1... | collective-permute-start | bytes 104 | tf_op jit(solution)/shard_map/ppermute | solution.py:159
  6.4 1.0 %copy-start.2 = (bf16[2,16,2,3584]{3,2,1,0:T(2,128)(2,1)S(1)}, bf16[2,16,2,3584]{3,2,1,0:T(2,128)(2,1)}, u32[]{:S(2)}) copy-start(bf16[2,16,2,3584]{3,2,1,0:T(2,128)(2,1)} %up.1) | copy-start | bytes 1376260
  7.4 0.9 %copy-start.3 = (bf16[2,16,2048]{2,1,0:T(8,128)(2,1)S(1)}, bf16[2,16,2048]{2,1,0:T(8,128)(2,1)}, u32[]{:S(2)}) copy-start(bf16[2,16,2048]{2,1,0:T(8,128)(2,1)} %down.1) | copy-start | bytes 393220
  8.3 0.7 %copy-start.4 = (s32[8]{0:T(128)S(1)}, s32[8]{0:T(128)}, u32[]{:S(2)}) copy-start(s32[8]{0:T(128)} %param.11) | copy-start | bytes 100
  10.6 12.6 %collective-permute-start.3 = (bf16[16,2048]{1,0:T(8,128)(2,1)S(1)}, bf16[16,2048]{1,0:T(8,128)(2,1)S(1)}, u32[]{:S(2)}, u32[]{:S(2)}) collective-permute-start(bf16[16,2048]{1,0:T(8,128)(2,1)S(1)} %get-tuple-element.51), channel_id=1, source_target_pairs={{0,12},{4,8},{8,4},{12,0},{1,13},{5,9},{9,5},{13,1},{2,14},{6,10},... | collective-permute-start | bytes 196616 | tf_op jit(solution)/shard_map/ppermute | solution.py:159
  13.6 14.8 %collective-permute-start.4 = (bf16[16,2048]{1,0:T(8,128)(2,1)S(1)}, bf16[16,2048]{1,0:T(8,128)(2,1)S(1)}, u32[]{:S(2)}, u32[]{:S(2)}) collective-permute-start(bf16[16,2048]{1,0:T(8,128)(2,1)S(1)} %get-tuple-element.52), channel_id=1, source_target_pairs={{0,8},{4,12},{8,0},{12,4},{1,9},{5,13},{9,1},{13,5},{2,10},{6,14},... | collective-permute-start | bytes 196616 | tf_op jit(solution)/shard_map/ppermute | solution.py:159
  13.6 14.8 %collective-permute-start.5 = (bf16[16,2048]{1,0:T(8,128)(2,1)S(1)}, bf16[16,2048]{1,0:T(8,128)(2,1)S(1)}, u32[]{:S(2)}, u32[]{:S(2)}) collective-permute-start(bf16[16,2048]{1,0:T(8,128)(2,1)S(1)} %get-tuple-element.53), channel_id=1, source_target_pairs={{0,4},{4,0},{8,12},{12,8},{1,5},{5,1},{9,13},{13,9},{2,6},{6,2},{1... | collective-permute-start | bytes 196616 | tf_op jit(solution)/shard_map/ppermute | solution.py:159
  15.1 22.3 %collective-permute-start.6 = (bf16[16,2,3584]{2,0,1:T(8,128)(2,1)S(1)}, bf16[16,2,3584]{2,0,1:T(8,128)(2,1)S(1)}, u32[]{:S(2)}, u32[]{:S(2)}) collective-permute-start(bf16[16,2,3584]{2,0,1:T(8,128)(2,1)S(1)} %copy.10), channel_id=1, source_target_pairs={{0,12},{4,8},{8,4},{12,0},{1,13},{5,9},{9,5},{13,1},{2,14},{6,10},... | collective-permute-start | bytes 688136 | tf_op jit(solution)/shard_map/ppermute | solution.py:159
  18.2 2.6 %copy-start.1 = (bf16[256,3584]{1,0:T(8,128)(2,1)S(1)}, bf16[256,3584]{1,0:T(8,128)(2,1)}, u32[]{:S(2)}) copy-start(bf16[256,3584]{1,0:T(8,128)(2,1)} %hidden) | copy-start | bytes 5505028
  20.8 27.8 %collective-permute-start.7 = (bf16[16,2,3584]{2,0,1:T(8,128)(2,1)S(1)}, bf16[16,2,3584]{2,0,1:T(8,128)(2,1)S(1)}, u32[]{:S(2)}, u32[]{:S(2)}) collective-permute-start(bf16[16,2,3584]{2,0,1:T(8,128)(2,1)S(1)} %copy.11), channel_id=1, source_target_pairs={{0,8},{4,12},{8,0},{12,4},{1,9},{5,13},{9,1},{13,5},{2,10},{6,14},... | collective-permute-start | bytes 688136 | tf_op jit(solution)/shard_map/ppermute | solution.py:159
  20.9 7.5 %copy-start = (bf16[256,2048]{1,0:T(8,128)(2,1)S(1)}, bf16[256,2048]{1,0:T(8,128)(2,1)}, u32[]{:S(2)}) copy-start(bf16[256,2048]{1,0:T(8,128)(2,1)} %acts.3) | copy-start | bytes 3145732
  23.3 25.4 %collective-permute-start.8 = (bf16[16,2,3584]{2,0,1:T(8,128)(2,1)S(1)}, bf16[16,2,3584]{2,0,1:T(8,128)(2,1)S(1)}, u32[]{:S(2)}, u32[]{:S(2)}) collective-permute-start(bf16[16,2,3584]{2,0,1:T(8,128)(2,1)S(1)} %copy.12), channel_id=1, source_target_pairs={{0,4},{4,0},{8,12},{12,8},{1,5},{5,1},{9,13},{13,9},{2,6},{6,2},{1... | collective-permute-start | bytes 688136 | tf_op jit(solution)/shard_map/ppermute | solution.py:159
  28.9 1.2 %collective-permute-start.14 = (f32[16,256]{1,0:T(8,128)S(1)}, f32[16,256]{1,0:T(8,128)S(1)}, u32[]{:S(2)}, u32[]{:S(2)}) collective-permute-start(f32[16,256]{1,0:T(8,128)S(1)} %shard_map.92), channel_id=1, source_target_pairs={{0,1},{1,0},{2,3},{3,2},{4,5},{5,4},{6,7},{7,6},{8,9},{9,8},{10,11... | collective-permute-start | bytes 49160 | tf_op jit(solution)/shard_map/ppermute | solution.py:207
  30.1 3.7 %collective-permute-start.15 = (f32[16,256]{1,0:T(8,128)S(1)}, f32[16,256]{1,0:T(8,128)S(1)}, u32[]{:S(2)}, u32[]{:S(2)}) collective-permute-start(f32[16,256]{1,0:T(8,128)S(1)} %add.8.low), channel_id=1, source_target_pairs={{0,2},{2,0},{1,3},{3,1},{4,6},{6,4},{5,7},{7,5},{8,10},{10,8},{9,1... | collective-permute-start | bytes 49160 | tf_op jit(solution)/shard_map/ppermute | solution.py:207
  34.6 23.1 %collective-permute-start.16 = (bf16[2,16,3584]{2,1,0:T(8,128)(2,1)S(1)}, bf16[2,16,3584]{2,1,0:T(8,128)(2,1)S(1)}, u32[]{:S(2)}, u32[]{:S(2)}) collective-permute-start(bf16[2,16,3584]{2,1,0:T(8,128)(2,1)S(1)} %get-tuple-element.73), channel_id=1, source_target_pairs={{0,12},{4,8},{8,4},{12,0},{1,13},{5,9},{9,5},{13,1},{2,14},{6,10},... | collective-permute-start | bytes 688136 | tf_op jit(solution)/shard_map/ppermute | solution.py:159
  37.4 23.6 %collective-permute-start.17 = (bf16[2,16,3584]{2,1,0:T(8,128)(2,1)S(1)}, bf16[2,16,3584]{2,1,0:T(8,128)(2,1)S(1)}, u32[]{:S(2)}, u32[]{:S(2)}) collective-permute-start(bf16[2,16,3584]{2,1,0:T(8,128)(2,1)S(1)} %get-tuple-element.74), channel_id=1, source_target_pairs={{0,8},{4,12},{8,0},{12,4},{1,9},{5,13},{9,1},{13,5},{2,10},{6,14},... | collective-permute-start | bytes 688136 | tf_op jit(solution)/shard_map/ppermute | solution.py:159
  37.4 23.6 %collective-permute-start.18 = (bf16[2,16,3584]{2,1,0:T(8,128)(2,1)S(1)}, bf16[2,16,3584]{2,1,0:T(8,128)(2,1)S(1)}, u32[]{:S(2)}, u32[]{:S(2)}) collective-permute-start(bf16[2,16,3584]{2,1,0:T(8,128)(2,1)S(1)} %get-tuple-element.75), channel_id=1, source_target_pairs={{0,4},{4,0},{8,12},{12,8},{1,5},{5,1},{9,13},{13,9},{2,6},{6,2},{1... | collective-permute-start | bytes 688136 | tf_op jit(solution)/shard_map/ppermute | solution.py:159
  49.9 1.2 %collective-permute-start.9 = (f32[16,256]{1,0:T(8,128)S(1)}, f32[16,256]{1,0:T(8,128)S(1)}, u32[]{:S(2)}, u32[]{:S(2)}) collective-permute-start(f32[16,256]{1,0:T(8,128)S(1)} %shard_map.88), channel_id=1, source_target_pairs={{0,1},{1,0},{2,3},{3,2},{4,5},{5,4},{6,7},{7,6},{8,9},{9,8},{10,11... | collective-permute-start | bytes 49160 | tf_op jit(solution)/shard_map/ppermute | solution.py:207
  51.1 3.7 %collective-permute-start.10 = (f32[16,256]{1,0:T(8,128)S(1)}, f32[16,256]{1,0:T(8,128)S(1)}, u32[]{:S(2)}, u32[]{:S(2)}) collective-permute-start(f32[16,256]{1,0:T(8,128)S(1)} %add.7.low), channel_id=1, source_target_pairs={{0,2},{2,0},{1,3},{3,1},{4,6},{6,4},{5,7},{7,5},{8,10},{10,8},{9,1... | collective-permute-start | bytes 49160 | tf_op jit(solution)/shard_map/ppermute | solution.py:207
  55.2 7.6 %collective-permute-start.11 = (bf16[16,2048]{1,0:T(8,128)(2,1)S(1)}, bf16[16,2048]{1,0:T(8,128)(2,1)S(1)}, u32[]{:S(2)}, u32[]{:S(2)}) collective-permute-start(bf16[16,2048]{1,0:T(8,128)(2,1)S(1)} %get-tuple-element.69), channel_id=1, source_target_pairs={{0,12},{4,8},{8,4},{12,0},{1,13},{5,9},{9,5},{13,1},{2,14},{6,10},... | collective-permute-start | bytes 196616 | tf_op jit(solution)/shard_map/ppermute | solution.py:159
  57.7 5.8 %collective-permute-start.12 = (bf16[16,2048]{1,0:T(8,128)(2,1)S(1)}, bf16[16,2048]{1,0:T(8,128)(2,1)S(1)}, u32[]{:S(2)}, u32[]{:S(2)}) collective-permute-start(bf16[16,2048]{1,0:T(8,128)(2,1)S(1)} %get-tuple-element.70), channel_id=1, source_target_pairs={{0,8},{4,12},{8,0},{12,4},{1,9},{5,13},{9,1},{13,5},{2,10},{6,14},... | collective-permute-start | bytes 196616 | tf_op jit(solution)/shard_map/ppermute | solution.py:159
  57.7 5.8 %collective-permute-start.13 = (bf16[16,2048]{1,0:T(8,128)(2,1)S(1)}, bf16[16,2048]{1,0:T(8,128)(2,1)S(1)}, u32[]{:S(2)}, u32[]{:S(2)}) collective-permute-start(bf16[16,2048]{1,0:T(8,128)(2,1)S(1)} %get-tuple-element.71), channel_id=1, source_target_pairs={{0,4},{4,0},{8,12},{12,8},{1,5},{5,1},{9,13},{13,9},{2,6},{6,2},{1... | collective-permute-start | bytes 196616 | tf_op jit(solution)/shard_map/ppermute | solution.py:159

commit v4 on v3

--- a/solution.py
+++ b/solution.py
@@ -42,8 +42,8 @@
     return me ^ k if count & (count - 1) == 0 else lax.rem(me + k, count)
 
 
-def bring(ids, down, up, ids_out, down_out, up_out, arrived):
-    pairs = ((ids, ids_out), (down, down_out), (up, up_out))
+def bring(ids, down, ids_out, down_out, arrived):
+    pairs = ((ids, ids_out), (down, down_out))
     copies = [pltpu.make_async_copy(a, b, arrived.at[i]) for i, (a, b) in enumerate(pairs)]
     for copy in copies:
         copy.start()
@@ -125,14 +125,12 @@
     out[...] = (adapter_scale * dot(wide[...], stack[...], 0, 0)).astype(BF)
 
 
-def held_sum_a(count, slots, *refs):
-    ids, parts, out = refs[:count], refs[count : 2 * count], refs[2 * count]
-    asked = [asked_slot(ids[k][...], slots) for k in range(count)]
-    for a in range(slots):
-        total = jnp.zeros(parts[0].shape, F32)
-        for k in range(count):
-            total = total + jnp.where(asked[k] == a, parts[k][...].astype(F32), 0.0)
-        out[a] = total
+def asked_weights(count, slots, *refs):
+    ids, out = refs[:count], refs[count]
+    for k in range(count):
+        asked = asked_slot(ids[k][...], slots)
+        for a in range(slots):
+            out[k, a] = jnp.full(out.shape[2:], (asked == a).astype(F32))
 
 
 def held_sum_b(count, slots, *refs):
@@ -166,18 +164,18 @@
         ids_from[k] = shift(ids, k)
     ids_from = [ids_from[k].reshape(1, -1) for k in order + [0]]
 
-    own_ids = ids.reshape(1, -1)
-    own_ids, own_down, own_up = on_chip(
+    own_ids, own_down = on_chip(
         bring,
-        [shape(own_ids.shape, ids.dtype), shape(down.shape, BF), shape(up.shape, BF)],
-        [pltpu.SemaphoreType.DMA((3,))],
-        in_specs=[pl.BlockSpec(memory_space=pl.ANY)] * 3,
-    )(own_ids, down, up)
+        [shape((1, ids.shape[0]), ids.dtype), shape(down.shape, BF)],
+        [pltpu.SemaphoreType.DMA((2,))],
+        in_specs=[pl.BlockSpec(memory_space=pl.ANY)] * 2,
+    )(ids.reshape(1, -1), down)
     ids_from[-1] = own_ids
+    up_by_gate = jnp.swapaxes(up, 1, 2)
     sends = on_chip(
         functools.partial(choose, T, slots),
-        [shape((rank, width), BF)] * T + [shape((rank, 2, units), BF)] * T,
-    )(*ids_from, own_down, own_up)
+        [shape((rank, width), BF)] * T + [shape((2, rank, units), BF)] * T,
+    )(*ids_from, own_down, up_by_gate)
     sends, saved, hidden = lax.optimization_barrier((sends, saved, hidden))
     down_from, up_from = {0: sends[T - 1]}, {0: sends[2 * T - 1]}
     for k in order:
@@ -185,7 +183,7 @@
     for k in order:
         up_from[k] = shift(sends[2 * T - 1 - k], -k)
     down_from = [down_from[k] for k in order + [0]]
-    up_from = [jnp.swapaxes(up_from[k], 0, 1) for k in order + [0]]
+    up_from = [up_from[k] for k in order + [0]]
 
     saved_by_gate = jnp.swapaxes(saved, 0, 1)
     grad_gate, grad_up = on_chip(
@@ -251,10 +249,12 @@
         part(held_sum_b, T, slots),
         shape((slots, rank, 2, units), F32),
     )(*ids_from, *[got_b[k] for k in order + [0]])
-    grad_a = on_chip(
-        part(held_sum_a, T, slots),
-        shape((slots, rank, width), F32),
-    )(*ids_from, *[got_a[k] for k in order + [0]])
+    weights = on_chip(
+        functools.partial(asked_weights, T, slots), shape((T, slots, rank, 1), F32)
+    )(*ids_from)
+    grad_a = sum(
+        weights[i] * got_a[k].astype(F32)[None] for i, k in enumerate(order + [0])
+    )
     return grad_acts, grad_a, grad_b
 
 

time: 64.8 us -> 64.5 us (level)
  Pallas kernels: 9.93 us -> 8.86 us
  other arithmetic: 0.02 us -> 0.9 us
    pallas_call x2, Pallas kernels: 1.45 us -> 0.38 us  [the longest x1 0.22 us: on_device(): on_chip(functools.partial(asked_weights, T, slots), shape((T, slots, rank...]
    add x0 -> x1, other arithmetic: none -> 0.84 us  [on_device(): sum((weights[i] * got_a[k].astype(F32)[None] for i, k in enumerate(order...]
    optimization_barrier x5 -> x1, local copies, waits for them, and re-layouts: 2.63 us -> 2.53 us  [on_device(): sends, saved, hidden = lax.optimization_barrier((sends, saved, hidden))]
    unnamed x10 -> x9, local copies, waits for them, and re-layouts: 2.59 us -> 2.63 us
  transfers between devices with their start and end apart: 19 -> 19, of which waited for: 8 -> 8; matrix products, arithmetic and copies ran while one was open for 4% -> 6% of each run, Pallas kernels for 13% -> 13%
where the time goes in v4:
time: 64.5 us; the launch traced here: 64.3 us
  starting transfers between devices  26.7 us (41%)
  waiting for transfers between devices  21.6 us (33%)
  Pallas kernels  8.86 us (14%)
  local copies, waits for them, and re-layouts  5.41 us (8%)
  other arithmetic  0.9 us (1%)
  between operations  0.82 us (1%)
    ppermute x15, starting transfers between devices, shift(): return lax.ppermute(x, 'tenant', [(i, i ^ abs(k)) for i in range(T)])  23.6 us
    ppermute x15, waiting for transfers between devices, shift(): return lax.ppermute(x, 'tenant', [(i, i ^ abs(k)) for i in range(T)])  15 us
    ppermute x4, waiting for transfers between devices, feature_sum(): lax.ppermute(x, axis, [(i, (i + k) % n) for i in range(n)])  6.61 us
    ppermute x4, starting transfers between devices, feature_sum(): lax.ppermute(x, axis, [(i, (i + k) % n) for i in range(n)])  3.12 us
    unnamed x9, local copies, waits for them, and re-layouts  2.63 us
    optimization_barrier x1, local copies, waits for them, and re-layouts, on_device(): sends, saved, hidden = lax.optimization_barrier((sends, saved, hidden))  2.53 us
    pallas_call x1, Pallas kernels, on_device(): on_chip(gated_grad, [shape((rows, units), BF)] * 2, grid=(8,), in_specs=[...  2.33 us
    pallas_call x1, Pallas kernels, on_device(): on_chip(part(held_sum_b, T, slots), shape((slots, rank, 2, units), F32))  1.7 us
  transfers between devices with their start and end apart: 19, of which 8 were waited for; matrix products, arithmetic and copies ran while one was open for 6% of the time, Pallas kernels for 13%

profile of v4, /device:TPU:0, one launch (start us, length us, event | category | flops | bytes accessed | tf_op | source)
XLA Modules:
  0.0 64.3 jit_solution(5864484000703042632)
XLA Ops:
  0.6 5.1 %collective-permute-start = (s32[8]{0:T(128)}, s32[8]{0:T(128)S(1)}, u32[]{:S(2)}, u32[]{:S(2)}) collective-permute-start(s32[8]{0:T(128)} %param.11), channel_id=1, source_target_pairs={{0,12},{4,8},{8,4},{12,0},{1,13},{5,9},{9,5},{13,1},{2,14},{6,10},... | collective-permute-start | bytes 104 | tf_op jit(solution)/shard_map/ppermute | solution.py:157
  5.7 0.6 collective-permute-start.2
  6.4 1.1 %copy.16 = bf16[2,16,2,3584]{3,1,2,0:T(8,128)(2,1)S(1)} copy(bf16[2,16,2,3584]{3,2,1,0:T(2,128)(2,1)} %param.10) | data formatting | bytes 917504 | tf_op args[4]
  7.5 0.0 copy-start.2
  7.5 0.9 %copy-done.2 = bf16[2,16,2048]{2,1,0:T(8,128)(2,1)S(1)} copy-done((bf16[2,16,2048]{2,1,0:T(8,128)(2,1)S(1)}, bf16[2,16,2048]{2,1,0:T(8,128)(2,1)}, u32[]{:S(2)}) %copy-start.2) | copy-done | bytes 131096
  8.4 0.7 %copy-done.3 = s32[8]{0:T(128)S(1)} copy-done((s32[8]{0:T(128)S(1)}, s32[8]{0:T(128)}, u32[]{:S(2)}) %copy-start.3) | copy-done | bytes 56
  9.0 0.2 shard_map.85
  9.2 0.0 collective-permute-done
  9.2 1.1 %collective-permute-done.1 = s32[8]{0:T(128)S(1)} collective-permute-done((s32[8]{0:T(128)}, s32[8]{0:T(128)S(1)}, u32[]{:S(2)}, u32[]{:S(2)}) %collective-permute-start.1) | collective-permute-done | bytes 64 | tf_op jit(solution)/shard_map/ppermute | solution.py:157
  10.3 0.0 collective-permute-done.2
  10.3 0.3 shard_map.86
  10.6 2.7 %collective-permute-start.3 = (bf16[16,2048]{1,0:T(8,128)(2,1)S(1)}, bf16[16,2048]{1,0:T(8,128)(2,1)S(1)}, u32[]{:S(2)}, u32[]{:S(2)}) collective-permute-start(bf16[16,2048]{1,0:T(8,128)(2,1)S(1)} %get-tuple-element.49), channel_id=1, source_target_pairs={{0,12},{4,8},{8,4},{12,0},{1,13},{5,9},{9,5},{13,1},{2,14},{6,10},... | collective-permute-start | bytes 196616 | tf_op jit(solution)/shard_map/ppermute | solution.py:157
  13.3 1.7 %collective-permute-start.5 = (bf16[16,2048]{1,0:T(8,128)(2,1)S(1)}, bf16[16,2048]{1,0:T(8,128)(2,1)S(1)}, u32[]{:S(2)}, u32[]{:S(2)}) collective-permute-start(bf16[16,2048]{1,0:T(8,128)(2,1)S(1)} %get-tuple-element.51), channel_id=1, source_target_pairs={{0,4},{4,0},{8,12},{12,8},{1,5},{5,1},{9,13},{13,9},{2,6},{6,2},{1... | collective-permute-start | bytes 196616 | tf_op jit(solution)/shard_map/ppermute | solution.py:157
  15.1 2.7 %collective-permute-start.6 = (bf16[2,16,3584]{2,1,0:T(8,128)(2,1)S(1)}, bf16[2,16,3584]{2,1,0:T(8,128)(2,1)S(1)}, u32[]{:S(2)}, u32[]{:S(2)}) collective-permute-start(bf16[2,16,3584]{2,1,0:T(8,128)(2,1)S(1)} %get-tuple-element.59), channel_id=1, source_target_pairs={{0,12},{4,8},{8,4},{12,0},{1,13},{5,9},{9,5},{13,1},{2,14},{6,10},... | collective-permute-start | bytes 688136 | tf_op jit(solution)/shard_map/ppermute | solution.py:157
  17.7 0.1 broadcast_in_dim.2
  17.8 0.1 reshape_reshape.3.row_holder
  17.9 2.5 %copy.15 = bf16[256,2,3584]{2,0,1:T(8,128)(2,1)S(1)} copy(bf16[256,2,3584]{2,1,0:T(2,128)(2,1)} %param.7) | data formatting | bytes 7340032 | tf_op jit(solution)/shard_map/optimization_barrier | solution.py:179
  20.4 0.1 collective-permute-start.7
  20.5 0.0 copy-start
  20.5 2.3 %shard_map.87 = (bf16[256,3584]{1,0:T(8,128)(2,1)S(1)}, bf16[256,3584]{1,0:T(8,128)(2,1)S(1)}) custom-call(bf16[2,256,3584]{2,1,0:T(8,128)(2,1)S(1)} %bitcast.10, bf16[256,3584]{1,0:T(8,128)(2,1)S(1)} %copy-done.1), custom_call_target="tpu_custom_call" | custom-call | flops 1 | bytes 1 | tf_op jit(solution)/shard_map/pallas_call | solution.py:189
  22.9 0.0 collective-permute-done.3.refs_0_
  22.9 1.8 %collective-permute-start.8 = (bf16[2,16,3584]{2,1,0:T(8,128)(2,1)S(1)}, bf16[2,16,3584]{2,1,0:T(8,128)(2,1)S(1)}, u32[]{:S(2)}, u32[]{:S(2)}) collective-permute-start(bf16[2,16,3584]{2,1,0:T(8,128)(2,1)S(1)} %get-tuple-element.61), channel_id=1, source_target_pairs={{0,4},{4,0},{8,12},{12,8},{1,5},{5,1},{9,13},{13,9},{2,6},{6,2},{1... | collective-permute-start | bytes 688136 | tf_op jit(solution)/shard_map/ppermute | solution.py:157
  24.6 3.7 %collective-permute-done.4.refs_1_ = bf16[16,2048]{1,0:T(8,128)(2,1)S(1)} collective-permute-done((bf16[16,2048]{1,0:T(8,128)(2,1)S(1)}, bf16[16,2048]{1,0:T(8,128)(2,1)S(1)}, u32[]{:S(2)}, u32[]{:S(2)}) %collective-permute-start.4) | collective-permute-done | bytes 65568 | tf_op jit(solution)/shard_map/ppermute | solution.py:157
  28.3 0.4 shard_map.92
  28.8 0.1 collective-permute-start.14
  28.8 1.2 %collective-permute-done.14 = f32[16,256]{1,0:T(8,128)S(1)} collective-permute-done((f32[16,256]{1,0:T(8,128)S(1)}, f32[16,256]{1,0:T(8,128)S(1)}, u32[]{:S(2)}, u32[]{:S(2)}) %collective-permute-start.14) | collective-permute-done | bytes 16416 | tf_op jit(solution)/shard_map/ppermute | solution.py:205
  30.0 1.5 %collective-permute-start.15 = (f32[16,256]{1,0:T(8,128)S(1)}, f32[16,256]{1,0:T(8,128)S(1)}, u32[]{:S(2)}, u32[]{:S(2)}) collective-permute-start(f32[16,256]{1,0:T(8,128)S(1)} %add.20.low), channel_id=1, source_target_pairs={{0,2},{2,0},{1,3},{3,1},{4,6},{6,4},{5,7},{7,5},{8,10},{10,8},{9,1... | collective-permute-start | bytes 49160 | tf_op jit(solution)/shard_map/ppermute | solution.py:205
  31.5 2.2 %collective-permute-done.15.more = f32[16,256]{1,0:T(8,128)S(1)} collective-permute-done((f32[16,256]{1,0:T(8,128)S(1)}, f32[16,256]{1,0:T(8,128)S(1)}, u32[]{:S(2)}, u32[]{:S(2)}) %collective-permute-start.15) | collective-permute-done | bytes 16416 | tf_op jit(solution)/shard_map/ppermute | solution.py:205
  33.8 0.7 %shard_map.93 = (bf16[2,16,3584]{2,1,0:T(8,128)(2,1)S(1)}, bf16[2,16,3584]{2,1,0:T(8,128)(2,1)S(1)}, bf16[2,16,3584]{2,1,0:T(8,128)(2,1)S(1)}, bf16[2,16,3584]{2,1,0:T(8,128)(2,1)S(1)}) custom-call(s32[1,256]{1,0:T(1,128)S(1)} %reshape_reshape.3.row_holder, f32[16,256]{1,0:T(8,128)S(1)} %add.20.low, f32[16,256]{1,0:T(8,128)S(1)} %collective-permute-done.15.more, ...), custom_call_target="tpu_custom_call" | custom-call | flops 1 | bytes 1 | tf_op jit(solution)/shard_map/pallas_call | solution.py:219
  34.5 3.3 %collective-permute-start.16 = (bf16[2,16,3584]{2,1,0:T(8,128)(2,1)S(1)}, bf16[2,16,3584]{2,1,0:T(8,128)(2,1)S(1)}, u32[]{:S(2)}, u32[]{:S(2)}) collective-permute-start(bf16[2,16,3584]{2,1,0:T(8,128)(2,1)S(1)} %get-tuple-element.71), channel_id=1, source_target_pairs={{0,12},{4,8},{8,4},{12,0},{1,13},{5,9},{9,5},{13,1},{2,14},{6,10},... | collective-permute-start | bytes 688136 | tf_op jit(solution)/shard_map/ppermute | solution.py:157
  37.8 0.0 collective-permute-start.17
  37.8 1.1 %collective-permute-start.18 = (bf16[2,16,3584]{2,1,0:T(8,128)(2,1)S(1)}, bf16[2,16,3584]{2,1,0:T(8,128)(2,1)S(1)}, u32[]{:S(2)}, u32[]{:S(2)}) collective-permute-start(bf16[2,16,3584]{2,1,0:T(8,128)(2,1)S(1)} %get-tuple-element.73), channel_id=1, source_target_pairs={{0,4},{4,0},{8,12},{12,8},{1,5},{5,1},{9,13},{13,9},{2,6},{6,2},{1... | collective-permute-start | bytes 688136 | tf_op jit(solution)/shard_map/ppermute | solution.py:157
  39.0 9.4 %collective-permute-done.7.refs_1_ = bf16[2,16,3584]{2,1,0:T(8,128)(2,1)S(1)} collective-permute-done((bf16[2,16,3584]{2,1,0:T(8,128)(2,1)S(1)}, bf16[2,16,3584]{2,1,0:T(8,128)(2,1)S(1)}, u32[]{:S(2)}, u32[]{:S(2)}) %collective-permute-start.7) | collective-permute-done | bytes 229408 | tf_op jit(solution)/shard_map/ppermute | solution.py:157
  48.4 0.0 collective-permute-done.8.refs_2_
  48.4 1.2 %shard_map.88 = f32[16,256]{1,0:T(8,128)S(1)} custom-call(s32[1,256]{1,0:T(1,128)S(1)} %reshape_reshape.3.row_holder, bf16[256,3584]{1,0:T(8,128)(2,1)S(1)} %get-tuple-element.57.gate, bf16[256,3584]{1,0:T(8,128)(2,1)S(1)} %get-tuple-element.58.up, bf16[2,16,3584]{2,1,0:T(8,128)(2,1)S(1)} %collective-permute-done.6.refs_0_, ...), custom_call_target="tpu_custom_call" | custom-call | flops 1 | bytes 1 | tf_op jit(solution)/shard_map/pallas_call | solution.py:225
  49.6 0.1 collective-permute-start.9
  49.7 1.2 %collective-permute-done.9 = f32[16,256]{1,0:T(8,128)S(1)} collective-permute-done((f32[16,256]{1,0:T(8,128)S(1)}, f32[16,256]{1,0:T(8,128)S(1)}, u32[]{:S(2)}, u32[]{:S(2)}) %collective-permute-start.9) | collective-permute-done | bytes 16416 | tf_op jit(solution)/shard_map/ppermute | solution.py:205
  50.9 1.5 %collective-permute-start.10 = (f32[16,256]{1,0:T(8,128)S(1)}, f32[16,256]{1,0:T(8,128)S(1)}, u32[]{:S(2)}, u32[]{:S(2)}) collective-permute-start(f32[16,256]{1,0:T(8,128)S(1)} %add.16.low), channel_id=1, source_target_pairs={{0,2},{2,0},{1,3},{3,1},{4,6},{6,4},{5,7},{7,5},{8,10},{10,8},{9,1... | collective-permute-start | bytes 49160 | tf_op jit(solution)/shard_map/ppermute | solution.py:205
  52.4 0.2 shard_map.90
  52.6 2.0 %collective-permute-done.10.more = f32[16,256]{1,0:T(8,128)S(1)} collective-permute-done((f32[16,256]{1,0:T(8,128)S(1)}, f32[16,256]{1,0:T(8,128)S(1)}, u32[]{:S(2)}, u32[]{:S(2)}) %collective-permute-start.10) | collective-permute-done | bytes 16416 | tf_op jit(solution)/shard_map/ppermute | solution.py:205
  54.6 0.3 shard_map.91
  54.9 2.5 %collective-permute-start.11 = (bf16[16,2048]{1,0:T(8,128)(2,1)S(1)}, bf16[16,2048]{1,0:T(8,128)(2,1)S(1)}, u32[]{:S(2)}, u32[]{:S(2)}) collective-permute-start(bf16[16,2048]{1,0:T(8,128)(2,1)S(1)} %get-tuple-element.67), channel_id=1, source_target_pairs={{0,12},{4,8},{8,4},{12,0},{1,13},{5,9},{9,5},{13,1},{2,14},{6,10},... | collective-permute-start | bytes 196616 | tf_op jit(solution)/shard_map/ppermute | solution.py:157
  57.4 2.0 %collective-permute-start.13 = (bf16[16,2048]{1,0:T(8,128)(2,1)S(1)}, bf16[16,2048]{1,0:T(8,128)(2,1)S(1)}, u32[]{:S(2)}, u32[]{:S(2)}) collective-permute-start(bf16[16,2048]{1,0:T(8,128)(2,1)S(1)} %get-tuple-element.69), channel_id=1, source_target_pairs={{0,4},{4,0},{8,12},{12,8},{1,5},{5,1},{9,13},{13,9},{2,6},{6,2},{1... | collective-permute-start | bytes 196616 | tf_op jit(solution)/shard_map/ppermute | solution.py:157
  59.4 0.1 slice_reduce_fusion.3
  59.5 1.4 %shard_map.89 = bf16[256,2048]{1,0:T(8,128)(2,1)} custom-call(s32[1,256]{1,0:T(1,128)S(1)} %reshape_reshape.3.row_holder, f32[16,256]{1,0:T(8,128)S(1)} %add.16.low, f32[16,256]{1,0:T(8,128)S(1)} %collective-permute-done.10.more, bf16[16,2048]{1,0:T(8,128)(2,1)S(1)} %collective-permute-done.3.refs_0_, bf16[16,2048]{1,0:T(8,128)(2,1)S(1)} %collective-permute-done.4.refs_1_, ...), custom_call_target="tpu_custom_call" | custom-call | flops 1 | bytes 1 | tf_op jit(solution)/shard_map/pallas_call | solution.py:236
  61.0 1.7 %shard_map.94 = f32[2,16,2,3584]{3,2,1,0:T(2,128)} custom-call(s32[1,8]{1,0:T(1,128)S(1)} %bitcast.14, s32[1,8]{1,0:T(1,128)S(1)} %bitcast.17, s32[1,8]{1,0:T(1,128)S(1)} %bitcast.20, s32[1,8]{1,0:T(1,128)S(1)} %get-tuple-element.39.refs_3_, bf16[2,16,3584]{2,1,0:T(8,128)(2,1)S(1)} %collective-permute-done.16.refs_4_, ...), custom_call_target="tpu_custom_call" | custom-call | flops 1 | bytes 1 | tf_op jit(solution)/shard_map/pallas_call | solution.py:248
  62.7 0.8 %collective-permute-done.12 = bf16[16,2048]{1,0:T(8,128)(2,1)S(1)} collective-permute-done((bf16[16,2048]{1,0:T(8,128)(2,1)S(1)}, bf16[16,2048]{1,0:T(8,128)(2,1)S(1)}, u32[]{:S(2)}, u32[]{:S(2)}) %collective-permute-start.12) | collective-permute-done | bytes 65568 | tf_op jit(solution)/shard_map/ppermute | solution.py:157
  63.5 0.8 %multiply_add_fusion = f32[2,16,2048]{2,1,0:T(8,128)} fusion(f32[16,2048]{1,0:T(8,128)S(1)} %convert_element_type.15, f32[2,16]{1,0:T(2,128)S(1)} %get-tuple-element.76, f32[16,2048]{1,0:T(8,128)S(1)} %convert_element_type.14, f32[2,16]{1,0:T(2,128)S(1)} %get-tuple-element.77, f32[16,2048]{1,0:T(8,128)S(1)} %convert_element_type.13, ...), kind=kLoop, calls=%fused_computation.2 | loop fusion | flops 458752 | bytes 786944 | tf_op jit(solution)/shard_map/add | solution.py:255
  (21 shorter events, 0.1 us)
Async XLA Ops:
  0.6 8.6 %collective-permute-start = (s32[8]{0:T(128)}, s32[8]{0:T(128)S(1)}, u32[]{:S(2)}, u32[]{:S(2)}) collective-permute-start(s32[8]{0:T(128)} %param.11), channel_id=1, source_target_pairs={{0,12},{4,8},{8,4},{12,0},{1,13},{5,9},{9,5},{13,1},{2,14},{6,10},... | collective-permute-start | bytes 104 | tf_op jit(solution)/shard_map/ppermute | solution.py:157
  5.7 4.6 %collective-permute-start.1 = (s32[8]{0:T(128)}, s32[8]{0:T(128)S(1)}, u32[]{:S(2)}, u32[]{:S(2)}) collective-permute-start(s32[8]{0:T(128)} %param.11), channel_id=1, source_target_pairs={{0,8},{4,12},{8,0},{12,4},{1,9},{5,13},{9,1},{13,5},{2,10},{6,14},... | collective-permute-start | bytes 104 | tf_op jit(solution)/shard_map/ppermute | solution.py:157
  5.7 4.6 %collective-permute-start.2 = (s32[8]{0:T(128)}, s32[8]{0:T(128)S(1)}, u32[]{:S(2)}, u32[]{:S(2)}) collective-permute-start(s32[8]{0:T(128)} %param.11), channel_id=1, source_target_pairs={{0,4},{4,0},{8,12},{12,8},{1,5},{5,1},{9,13},{13,9},{2,6},{6,2},{1... | collective-permute-start | bytes 104 | tf_op jit(solution)/shard_map/ppermute | solution.py:157
  7.5 0.9 %copy-start.2 = (bf16[2,16,2048]{2,1,0:T(8,128)(2,1)S(1)}, bf16[2,16,2048]{2,1,0:T(8,128)(2,1)}, u32[]{:S(2)}) copy-start(bf16[2,16,2048]{2,1,0:T(8,128)(2,1)} %down.1) | copy-start | bytes 393220
  8.4 0.7 %copy-start.3 = (s32[8]{0:T(128)S(1)}, s32[8]{0:T(128)}, u32[]{:S(2)}) copy-start(s32[8]{0:T(128)} %param.11) | copy-start | bytes 100
  10.6 12.2 %collective-permute-start.3 = (bf16[16,2048]{1,0:T(8,128)(2,1)S(1)}, bf16[16,2048]{1,0:T(8,128)(2,1)S(1)}, u32[]{:S(2)}, u32[]{:S(2)}) collective-permute-start(bf16[16,2048]{1,0:T(8,128)(2,1)S(1)} %get-tuple-element.49), channel_id=1, source_target_pairs={{0,12},{4,8},{8,4},{12,0},{1,13},{5,9},{9,5},{13,1},{2,14},{6,10},... | collective-permute-start | bytes 196616 | tf_op jit(solution)/shard_map/ppermute | solution.py:157
  13.3 15.0 %collective-permute-start.4 = (bf16[16,2048]{1,0:T(8,128)(2,1)S(1)}, bf16[16,2048]{1,0:T(8,128)(2,1)S(1)}, u32[]{:S(2)}, u32[]{:S(2)}) collective-permute-start(bf16[16,2048]{1,0:T(8,128)(2,1)S(1)} %get-tuple-element.50), channel_id=1, source_target_pairs={{0,8},{4,12},{8,0},{12,4},{1,9},{5,13},{9,1},{13,5},{2,10},{6,14},... | collective-permute-start | bytes 196616 | tf_op jit(solution)/shard_map/ppermute | solution.py:157
  13.3 15.0 %collective-permute-start.5 = (bf16[16,2048]{1,0:T(8,128)(2,1)S(1)}, bf16[16,2048]{1,0:T(8,128)(2,1)S(1)}, u32[]{:S(2)}, u32[]{:S(2)}) collective-permute-start(bf16[16,2048]{1,0:T(8,128)(2,1)S(1)} %get-tuple-element.51), channel_id=1, source_target_pairs={{0,4},{4,0},{8,12},{12,8},{1,5},{5,1},{9,13},{13,9},{2,6},{6,2},{1... | collective-permute-start | bytes 196616 | tf_op jit(solution)/shard_map/ppermute | solution.py:157
  15.1 22.8 %collective-permute-start.6 = (bf16[2,16,3584]{2,1,0:T(8,128)(2,1)S(1)}, bf16[2,16,3584]{2,1,0:T(8,128)(2,1)S(1)}, u32[]{:S(2)}, u32[]{:S(2)}) collective-permute-start(bf16[2,16,3584]{2,1,0:T(8,128)(2,1)S(1)} %get-tuple-element.59), channel_id=1, source_target_pairs={{0,12},{4,8},{8,4},{12,0},{1,13},{5,9},{9,5},{13,1},{2,14},{6,10},... | collective-permute-start | bytes 688136 | tf_op jit(solution)/shard_map/ppermute | solution.py:157
  17.9 2.6 %copy-start.1 = (bf16[256,3584]{1,0:T(8,128)(2,1)S(1)}, bf16[256,3584]{1,0:T(8,128)(2,1)}, u32[]{:S(2)}) copy-start(bf16[256,3584]{1,0:T(8,128)(2,1)} %hidden) | copy-start | bytes 5505028
  20.4 28.0 %collective-permute-start.7 = (bf16[2,16,3584]{2,1,0:T(8,128)(2,1)S(1)}, bf16[2,16,3584]{2,1,0:T(8,128)(2,1)S(1)}, u32[]{:S(2)}, u32[]{:S(2)}) collective-permute-start(bf16[2,16,3584]{2,1,0:T(8,128)(2,1)S(1)} %get-tuple-element.60), channel_id=1, source_target_pairs={{0,8},{4,12},{8,0},{12,4},{1,9},{5,13},{9,1},{13,5},{2,10},{6,14},... | collective-permute-start | bytes 688136 | tf_op jit(solution)/shard_map/ppermute | solution.py:157
  20.5 7.8 %copy-start = (bf16[256,2048]{1,0:T(8,128)(2,1)S(1)}, bf16[256,2048]{1,0:T(8,128)(2,1)}, u32[]{:S(2)}) copy-start(bf16[256,2048]{1,0:T(8,128)(2,1)} %acts.3) | copy-start | bytes 3145732
  22.9 25.5 %collective-permute-start.8 = (bf16[2,16,3584]{2,1,0:T(8,128)(2,1)S(1)}, bf16[2,16,3584]{2,1,0:T(8,128)(2,1)S(1)}, u32[]{:S(2)}, u32[]{:S(2)}) collective-permute-start(bf16[2,16,3584]{2,1,0:T(8,128)(2,1)S(1)} %get-tuple-element.61), channel_id=1, source_target_pairs={{0,4},{4,0},{8,12},{12,8},{1,5},{5,1},{9,13},{13,9},{2,6},{6,2},{1... | collective-permute-start | bytes 688136 | tf_op jit(solution)/shard_map/ppermute | solution.py:157
  28.8 1.2 %collective-permute-start.14 = (f32[16,256]{1,0:T(8,128)S(1)}, f32[16,256]{1,0:T(8,128)S(1)}, u32[]{:S(2)}, u32[]{:S(2)}) collective-permute-start(f32[16,256]{1,0:T(8,128)S(1)} %shard_map.92), channel_id=1, source_target_pairs={{0,1},{1,0},{2,3},{3,2},{4,5},{5,4},{6,7},{7,6},{8,9},{9,8},{10,11... | collective-permute-start | bytes 49160 | tf_op jit(solution)/shard_map/ppermute | solution.py:205
  30.0 3.7 %collective-permute-start.15 = (f32[16,256]{1,0:T(8,128)S(1)}, f32[16,256]{1,0:T(8,128)S(1)}, u32[]{:S(2)}, u32[]{:S(2)}) collective-permute-start(f32[16,256]{1,0:T(8,128)S(1)} %add.20.low), channel_id=1, source_target_pairs={{0,2},{2,0},{1,3},{3,1},{4,6},{6,4},{5,7},{7,5},{8,10},{10,8},{9,1... | collective-permute-start | bytes 49160 | tf_op jit(solution)/shard_map/ppermute | solution.py:205
  34.5 22.9 %collective-permute-start.16 = (bf16[2,16,3584]{2,1,0:T(8,128)(2,1)S(1)}, bf16[2,16,3584]{2,1,0:T(8,128)(2,1)S(1)}, u32[]{:S(2)}, u32[]{:S(2)}) collective-permute-start(bf16[2,16,3584]{2,1,0:T(8,128)(2,1)S(1)} %get-tuple-element.71), channel_id=1, source_target_pairs={{0,12},{4,8},{8,4},{12,0},{1,13},{5,9},{9,5},{13,1},{2,14},{6,10},... | collective-permute-start | bytes 688136 | tf_op jit(solution)/shard_map/ppermute | solution.py:157
  37.8 23.1 %collective-permute-start.17 = (bf16[2,16,3584]{2,1,0:T(8,128)(2,1)S(1)}, bf16[2,16,3584]{2,1,0:T(8,128)(2,1)S(1)}, u32[]{:S(2)}, u32[]{:S(2)}) collective-permute-start(bf16[2,16,3584]{2,1,0:T(8,128)(2,1)S(1)} %get-tuple-element.72), channel_id=1, source_target_pairs={{0,8},{4,12},{8,0},{12,4},{1,9},{5,13},{9,1},{13,5},{2,10},{6,14},... | collective-permute-start | bytes 688136 | tf_op jit(solution)/shard_map/ppermute | solution.py:157
  37.8 23.1 %collective-permute-start.18 = (bf16[2,16,3584]{2,1,0:T(8,128)(2,1)S(1)}, bf16[2,16,3584]{2,1,0:T(8,128)(2,1)S(1)}, u32[]{:S(2)}, u32[]{:S(2)}) collective-permute-start(bf16[2,16,3584]{2,1,0:T(8,128)(2,1)S(1)} %get-tuple-element.73), channel_id=1, source_target_pairs={{0,4},{4,0},{8,12},{12,8},{1,5},{5,1},{9,13},{13,9},{2,6},{6,2},{1... | collective-permute-start | bytes 688136 | tf_op jit(solution)/shard_map/ppermute | solution.py:157
  49.6 1.2 %collective-permute-start.9 = (f32[16,256]{1,0:T(8,128)S(1)}, f32[16,256]{1,0:T(8,128)S(1)}, u32[]{:S(2)}, u32[]{:S(2)}) collective-permute-start(f32[16,256]{1,0:T(8,128)S(1)} %shard_map.88), channel_id=1, source_target_pairs={{0,1},{1,0},{2,3},{3,2},{4,5},{5,4},{6,7},{7,6},{8,9},{9,8},{10,11... | collective-permute-start | bytes 49160 | tf_op jit(solution)/shard_map/ppermute | solution.py:205
  50.9 3.7 %collective-permute-start.10 = (f32[16,256]{1,0:T(8,128)S(1)}, f32[16,256]{1,0:T(8,128)S(1)}, u32[]{:S(2)}, u32[]{:S(2)}) collective-permute-start(f32[16,256]{1,0:T(8,128)S(1)} %add.16.low), channel_id=1, source_target_pairs={{0,2},{2,0},{1,3},{3,1},{4,6},{6,4},{5,7},{7,5},{8,10},{10,8},{9,1... | collective-permute-start | bytes 49160 | tf_op jit(solution)/shard_map/ppermute | solution.py:205
  54.9 7.7 %collective-permute-start.11 = (bf16[16,2048]{1,0:T(8,128)(2,1)S(1)}, bf16[16,2048]{1,0:T(8,128)(2,1)S(1)}, u32[]{:S(2)}, u32[]{:S(2)}) collective-permute-start(bf16[16,2048]{1,0:T(8,128)(2,1)S(1)} %get-tuple-element.67), channel_id=1, source_target_pairs={{0,12},{4,8},{8,4},{12,0},{1,13},{5,9},{9,5},{13,1},{2,14},{6,10},... | collective-permute-start | bytes 196616 | tf_op jit(solution)/shard_map/ppermute | solution.py:157
  57.4 6.1 %collective-permute-start.12 = (bf16[16,2048]{1,0:T(8,128)(2,1)S(1)}, bf16[16,2048]{1,0:T(8,128)(2,1)S(1)}, u32[]{:S(2)}, u32[]{:S(2)}) collective-permute-start(bf16[16,2048]{1,0:T(8,128)(2,1)S(1)} %get-tuple-element.68), channel_id=1, source_target_pairs={{0,8},{4,12},{8,0},{12,4},{1,9},{5,13},{9,1},{13,5},{2,10},{6,14},... | collective-permute-start | bytes 196616 | tf_op jit(solution)/shard_map/ppermute | solution.py:157
  57.4 6.1 %collective-permute-start.13 = (bf16[16,2048]{1,0:T(8,128)(2,1)S(1)}, bf16[16,2048]{1,0:T(8,128)(2,1)S(1)}, u32[]{:S(2)}, u32[]{:S(2)}) collective-permute-start(bf16[16,2048]{1,0:T(8,128)(2,1)S(1)} %get-tuple-element.69), channel_id=1, source_target_pairs={{0,4},{4,0},{8,12},{12,8},{1,5},{5,1},{9,13},{13,9},{2,6},{6,2},{1... | collective-permute-start | bytes 196616 | tf_op jit(solution)/shard_map/ppermute | solution.py:157
